TPU v7x, 32 devices: a whole 2x2x4 slice. The times are simulated.
32 devices in a mesh: replica: 16 (over z, y, x), tensor: 2 (over core).
Axes of the slice: x: 2, y: 2, z: 4, core: 2. Of those that a mesh axis runs over, the one named last changes fastest.
Arguments:
- lengths: int32 [256], replicated, may hold values from 1 to 254, as said below
- page_table: int32 [256, 2], P('replica'), may hold values from 0 to 31, as said below
- key_pool: bfloat16 [512, 128, 1024], P('replica', None, 'tensor'), may hold values from -4 to 4
- value_pool: bfloat16 [512, 128, 1024], P('replica', None, 'tensor'), may hold values from -5 to 5
- queries: bfloat16 [2, 256, 4096], P(None, 'replica', 'tensor'), may hold values from -80 to 80
- new_keys: bfloat16 [2, 256, 1024], P(None, 'replica', 'tensor'), may hold values from -4 to 4
- new_values: bfloat16 [2, 256, 1024], P(None, 'replica', 'tensor'), may hold values from -5 to 5
- conv_state: float32 [256, 3, 8192], P('replica', None, 'tensor'), may hold values from -5 to 5
- ssm_state: float32 [256, 16, 8192], P('replica', None, 'tensor'), may hold values from -5 to 5
- mamba_x: bfloat16 [2, 256, 8192], P(None, 'replica', 'tensor'), may hold values from -5 to 5
- mamba_z: bfloat16 [2, 256, 8192], P(None, 'replica', 'tensor'), may hold values from -5 to 5
- conv_weight: float32 [4, 8192], P(None, 'tensor'), may hold values from -3 to 3
- conv_bias: float32 [8192], P('tensor'), may hold values from -3 to 3
- dt_down: bfloat16 [8192, 256], P('tensor'), may hold values from -0.0625 to 0.0625
- bc_proj: bfloat16 [8192, 32], P('tensor'), may hold values from -0.0625 to 0.0625
- dt_up: bfloat16 [256, 8192], P(None, 'tensor'), may hold values from -0.375 to 0.375
- dt_bias: float32 [8192], P('tensor'), may hold values from -3 to 0
- a_log: float32 [16, 8192], P(None, 'tensor'), may hold values from 0 to 2.77
- skip_d: float32 [8192], P('tensor'), may hold values from 0.5 to 2
- moves: int32 [128, 2], replicated, may hold values from 0 to 255, as said below
Outputs:
- attention: bfloat16 [2, 256, 4096], P(None, 'replica', 'tensor')
- mamba_out: bfloat16 [2, 256, 8192], P(None, 'replica', 'tensor')
- final_ssm: float32 [256, 16, 8192], P('replica', None, 'tensor')
- final_conv: float32 [256, 3, 8192], P('replica', None, 'tensor')
Inputs may be any that keep to these rules, and one draw needn't show every extreme that they name: `lengths`: each replica has one request of the longest length. `page_table`: the rows of the 16 requests of one replica name each of that replica's 32 pages once. `moves`: rows r * 8 to r * 8 + 7 are the 8 requests that leave replica r, each to another replica, no two to the same one; every replica receives 8 requests, from 8 different replicas, into exactly the slots that its own leaving requests free; the j-th row of every replica goes the same number of replicas further along, counted modulo the number of replicas; one of these numbers is 1 and another is half the number of replicas.
All inputs are finite; a program needn't handle non-finite values.
Results may differ from a plain program's by a relative error of at most 0.013.
Values may be sent and summed in bfloat16 or wider, within the bound.
A program may use at most 128 MiB of HBM per device.

v0:
```python
import math

import jax
import jax.numpy as jnp
from jax import lax
from jax.sharding import PartitionSpec as P

HD = 128


def attend(query_rows, key_rows, value_rows, last_pos):
    rows_count = query_rows.shape[0]
    key_span = key_rows.shape[1]
    kv_heads = key_rows.shape[2] // HD
    group_size = query_rows.shape[1] // key_rows.shape[2]
    query_heads = query_rows.reshape(rows_count, kv_heads, group_size, HD)
    key_heads = key_rows.reshape(rows_count, key_span, kv_heads, HD)
    value_heads = value_rows.reshape(rows_count, key_span, kv_heads, HD)
    scores = jnp.einsum(
        "skgd,spkd->skgp", query_heads, key_heads, preferred_element_type=jnp.float32
    ) * (1.0 / math.sqrt(HD))
    visible = jnp.arange(key_span)[None, :] <= last_pos[:, None]
    scores = jnp.where(visible[:, None, None, :], scores, -1e30)
    largest = jnp.max(scores, axis=-1, keepdims=True)
    exponent = jnp.exp(scores - largest)
    weights = (exponent / jnp.sum(exponent, axis=-1, keepdims=True)).astype(jnp.bfloat16)
    attended = jnp.einsum(
        "skgp,spkd->skgd", weights, value_heads, preferred_element_type=jnp.float32
    )
    return attended.astype(jnp.bfloat16).reshape(rows_count, query_rows.shape[1])


def mamba_step(conv_prev, state_prev, x_in, z_in, params):
    conv_weight, conv_bias, dt_down, bc_proj, dt_up, dt_bias, a_log, skip_d = params
    window = jnp.concatenate([conv_prev, x_in.astype(jnp.float32)[:, None, :]], axis=1)
    conv_out = jax.nn.silu(jnp.sum(window * conv_weight[None], axis=1) + conv_bias)
    mixed_in = conv_out.astype(jnp.bfloat16)
    low_rank, bc_terms = lax.psum(
        (
            jnp.dot(mixed_in, dt_down, preferred_element_type=jnp.float32),
            jnp.dot(mixed_in, bc_proj, preferred_element_type=jnp.float32),
        ),
        "tensor",
    )
    dt_step = jax.nn.softplus(
        jnp.dot(low_rank.astype(jnp.bfloat16), dt_up, preferred_element_type=jnp.float32) + dt_bias
    )
    state_count = a_log.shape[0]
    b_in = bc_terms[:, :state_count]
    c_out = bc_terms[:, state_count:]
    inputs_wide = mixed_in.astype(jnp.float32)
    decay_rate = jnp.exp(-dt_step[:, None, :] * jnp.exp(a_log)[None])
    state_new = (
        decay_rate * state_prev + dt_step[:, None, :] * b_in[:, :, None] * inputs_wide[:, None, :]
    )
    output = (jnp.sum(c_out[:, :, None] * state_new, axis=1) + skip_d * inputs_wide) * jax.nn.silu(
        z_in.astype(jnp.float32)
    )
    return (output.astype(jnp.bfloat16), window[:, 1:], state_new)


def keep_where(flags, moved, staying):
    return jnp.where(flags.reshape((flags.shape[0],) + (1,) * (staying.ndim - 1)), moved, staying)


def shards(
    lengths,
    page_table,
    key_pool,
    value_pool,
    queries,
    new_keys,
    new_values,
    conv_state,
    ssm_state,
    mamba_x,
    mamba_z,
    conv_weight,
    conv_bias,
    dt_down,
    bc_proj,
    dt_up,
    dt_bias,
    a_log,
    skip_d,
    moves,
):
    params = (conv_weight, conv_bias, dt_down, bc_proj, dt_up, dt_bias, a_log, skip_d)
    replica = lax.axis_index("replica")
    replicas = lax.axis_size("replica")
    slot_count = page_table.shape[0]
    span_total = page_table.shape[1] * key_pool.shape[1]
    leaving_count = moves.shape[0] // replicas
    slot_ids = jnp.arange(slot_count, dtype=jnp.int32)
    own_slots = replica * slot_count + slot_ids
    own_lengths = lax.dynamic_slice_in_dim(lengths, replica * slot_count, slot_count)
    key_cache = (
        key_pool[page_table]
        .reshape(slot_count, span_total, key_pool.shape[2])
        .at[slot_ids, own_lengths]
        .set(new_keys[0])
    )
    value_cache = (
        value_pool[page_table]
        .reshape(slot_count, span_total, value_pool.shape[2])
        .at[slot_ids, own_lengths]
        .set(new_values[0])
    )
    attention_one = attend(queries[0], key_cache, value_cache, own_lengths)
    mamba_one, conv_one, state_one = mamba_step(
        conv_state, ssm_state, mamba_x[0], mamba_z[0], params
    )
    outgoing = lax.dynamic_slice_in_dim(moves, replica * leaving_count, leaving_count, 0)
    leave_slot = outgoing[:, 0] - replica * slot_count
    leave_dest = outgoing[:, 1] // slot_count
    matches = moves[None, :, 1] == own_slots[:, None]
    arrived = jnp.any(matches, axis=1)
    source_slot = jnp.where(
        arrived, jnp.sum(jnp.where(matches, moves[None, :, 0], 0), axis=1), own_slots
    )
    source_rep = source_slot // slot_count
    later_lengths = lengths[source_slot]

    def pack_moving(local_rows):
        empty = jnp.zeros((replicas,) + local_rows.shape[1:], local_rows.dtype)
        return empty.at[leave_dest].set(local_rows[leave_slot])

    def take_arrived(received, local_rows):
        return keep_where(arrived, received[source_rep], local_rows)

    conv_got, state_got = (
        lax.all_to_all(pack_moving(conv_one), "replica", split_axis=0, concat_axis=0, tiled=True),
        lax.all_to_all(pack_moving(state_one), "replica", split_axis=0, concat_axis=0, tiled=True),
    )
    conv_next = take_arrived(conv_got, conv_one)
    state_next = take_arrived(state_got, state_one)
    mamba_two, final_conv, final_ssm = mamba_step(
        conv_next, state_next, mamba_x[1], mamba_z[1], params
    )
    keys_got, values_got = (
        lax.all_to_all(pack_moving(key_cache), "replica", split_axis=0, concat_axis=0, tiled=True),
        lax.all_to_all(
            pack_moving(value_cache), "replica", split_axis=0, concat_axis=0, tiled=True
        ),
    )
    moved_keys_all = take_arrived(keys_got, key_cache)
    moved_values_all = take_arrived(values_got, value_cache)
    later_keys = moved_keys_all.at[slot_ids, later_lengths + 1].set(new_keys[1])
    later_values = moved_values_all.at[slot_ids, later_lengths + 1].set(new_values[1])
    attention_two = attend(queries[1], later_keys, later_values, later_lengths + 1)
    return (
        jnp.stack([attention_one, attention_two]),
        jnp.stack([mamba_one, mamba_two]),
        final_ssm,
        final_conv,
    )


def solution(mesh):
    in_specs = (
        P(),
        P("replica", None),
        P("replica", None, "tensor"),
        P("replica", None, "tensor"),
        P(None, "replica", "tensor"),
        P(None, "replica", "tensor"),
        P(None, "replica", "tensor"),
        P("replica", None, "tensor"),
        P("replica", None, "tensor"),
        P(None, "replica", "tensor"),
        P(None, "replica", "tensor"),
        P(None, "tensor"),
        P("tensor"),
        P("tensor", None),
        P("tensor", None),
        P(None, "tensor"),
        P("tensor"),
        P(None, "tensor"),
        P("tensor"),
        P(),
    )
    out_specs = (
        P(None, "replica", "tensor"),
        P(None, "replica", "tensor"),
        P("replica", None, "tensor"),
        P("replica", None, "tensor"),
    )
    return jax.shard_map(shards, mesh=mesh, in_specs=in_specs, out_specs=out_specs, check_vma=False)
```

profile of v0, /device:TPU:14, one launch (start us, length us, event | category | flops | bytes accessed | tf_op | source)
XLA Modules:
  0.0 349.2 jit_solution(16012826673359547564)
XLA Ops:
  0.7 0.9 constant_dynamic-slice_fusion
  1.6 1.0 fusion.45
  2.9 1.7 copy.61
  4.6 1.5 fusion.15
  6.1 2.8 gather_fusion.7
  8.9 1.2 broadcast_in_dim.74
  10.2 2.7 scatter_fusion.6
  12.9 7.2 %all-to-all-start.2 = ((f32[16,3,4096]{2,1,0:T(4,128)}), f32[16,3,4096]{2,1,0:T(4,128)}, u32[]{:S(2)}, u32[]{:S(2)}) async-start(f32[16,3,4096]{2,1,0:T(4,128)} %scatter_fusion.6), calls=%async_computation.2 | async-start | bytes 2097152 | tf_op jit(solution)/shard_map/all_to_all | solution.py:132
  20.3 4.9 %gather_fusion = bf16[32,128,512]{2,1,0:T(8,128)(2,1)} fusion(bf16[32,128,512]{2,1,0:T(8,128)(2,1)} %param.22, s32[1024]{0:T(1024)S(1)} %pad_clamp_fusion.3), kind=kCustom, calls=%fused_computation | custom fusion | bytes 8388736 | tf_op jit(solution)/shard_map/gather | solution.py:98
  25.2 0.7 fusion.41
  25.9 1.3 slice_bitcast_fusion.1
  27.2 2.6 scatter_fusion
  29.8 4.4 %gather_fusion.3 = bf16[8,256,512]{2,1,0:T(8,128)(2,1)} fusion(bf16[16,256,512]{2,1,0:T(8,128)(2,1)} %scatter_fusion, s32[1024]{0:T(1024)} %copy-done.28), kind=kCustom, calls=%fused_computation.3 | custom fusion | bytes 4194336 | tf_op jit(solution)/shard_map/gather | solution.py:126
  34.2 2.4 broadcast.391.clone
  36.6 5.7 %scatter_fusion.2 = bf16[16,256,512]{2,1,0:T(8,128)(2,1)} fusion(bf16[16,256,512]{2,1,0:T(8,128)(2,1)} %broadcast.391.clone, s32[8]{0:T(128)S(1)} %copy-done.26, bf16[8,256,512]{2,1,0:T(8,128)(2,1)} %gather_fusion.3), kind=kCustom, calls=%fused_computation.13 | custom fusion | bytes 6291488 | tf_op jit(solution)/shard_map/scatter | solution.py:126
  42.3 2.3 all-to-all-done.2
  44.6 5.8 %all-to-all-start = ((bf16[16,256,512]{2,1,0:T(8,128)(2,1)}), bf16[16,256,512]{2,1,0:T(8,128)(2,1)}, u32[]{:S(2)}, u32[]{:S(2)}) async-start(bf16[16,256,512]{2,1,0:T(8,128)(2,1)} %scatter_fusion.2), calls=%async_computation | async-start | bytes 8388608 | tf_op jit(solution)/shard_map/all_to_all | solution.py:141
  50.4 5.0 %gather_fusion.1 = bf16[32,128,512]{2,1,0:T(8,128)(2,1)} fusion(bf16[32,128,512]{2,1,0:T(8,128)(2,1)} %param.23, s32[1024]{0:T(1024)S(1)} %pad_clamp_fusion.3), kind=kCustom, calls=%fused_computation.1 | custom fusion | bytes 8388736 | tf_op jit(solution)/shard_map/gather | solution.py:104
  55.4 1.3 slice_bitcast_fusion
  56.8 2.6 scatter_fusion.1
  59.4 4.3 %gather_fusion.5 = bf16[8,256,512]{2,1,0:T(8,128)(2,1)} fusion(bf16[16,256,512]{2,1,0:T(8,128)(2,1)} %scatter_fusion.1, s32[1024]{0:T(1024)} %copy-done.28), kind=kCustom, calls=%fused_computation.5 | custom fusion | bytes 4194336 | tf_op jit(solution)/shard_map/gather | solution.py:126
  63.7 2.4 broadcast.391.clone.1
  66.1 5.8 %scatter_fusion.4 = bf16[16,256,512]{2,1,0:T(8,128)(2,1)} fusion(bf16[16,256,512]{2,1,0:T(8,128)(2,1)} %broadcast.391.clone.1, s32[8]{0:T(128)S(1)} %copy-done.26, bf16[8,256,512]{2,1,0:T(8,128)(2,1)} %gather_fusion.5), kind=kCustom, calls=%fused_computation.15 | custom fusion | bytes 6291488 | tf_op jit(solution)/shard_map/scatter | solution.py:126
  71.8 69.8 %all-to-all-done = bf16[16,256,512]{2,1,0:T(8,128)(2,1)} async-done(((bf16[16,256,512]{2,1,0:T(8,128)(2,1)}), bf16[16,256,512]{2,1,0:T(8,128)(2,1)}, u32[]{:S(2)}, u32[]{:S(2)}) %all-to-all-start) | async-done | bytes 4194336 | tf_op jit(solution)/shard_map/all_to_all | solution.py:141
  141.6 5.2 %all-to-all-start.1 = ((bf16[16,256,512]{2,1,0:T(8,128)(2,1)}), bf16[16,256,512]{2,1,0:T(8,128)(2,1)}, u32[]{:S(2)}, u32[]{:S(2)}) async-start(bf16[16,256,512]{2,1,0:T(8,128)(2,1)} %scatter_fusion.4), calls=%async_computation.1 | async-start | bytes 8388608 | tf_op jit(solution)/shard_map/all_to_all | solution.py:142
  146.8 1.7 exp.68
  149.4 1.0 fusion.24
  150.4 3.3 gather_fusion.8
  153.7 2.1 broadcast_select_fusion.2
  155.8 3.3 fusion.11
  159.1 0.7 copy-done.6
  159.8 0.8 fusion.43
  161.8 4.1 %all-reduce = (f32[16,32]{1,0:T(8,128)S(1)}, bf16[16,256]{1,0:T(8,128)(2,1)S(1)}, f32[16,32]{1,0:T(8,128)S(1)}, bf16[16,256]{1,0:T(8,128)(2,1)}) all-reduce(f32[16,32]{1,0:T(8,128)S(1)} %fusion.53, f32[16,256]{1,0:T(8,128)S(1)} %fusion.54, f32[16,32]{1,0:T(8,128)S(1)} %fusion.55, ...), channel_id=1, replica_groups=mesh['replica'=16,'tensor'=2] {'tensor'}, use_global_device_ids=true, to_apply=%region_13.14 | all-reduce | flops 9216 | bytes 57344 | tf_op jit(solution)/shard_map/psum | solution.py:38
  166.5 5.3 %multiply_reduce_fusion.1 = (f32[16,4096]{1,0:T(8,128)}, f32[16,16,4096]{2,1,0:T(8,128)}) fusion(f32[16,16]{1,0:T(8,128)S(1)} %get-tuple-element.47, f32[16,4096]{1,0:T(8,128)S(1)} %get-tuple-element.44, f32[16,16]{1,0:T(8,128)S(1)} %get-tuple-element.46, f32[16,4096]{1,0:T(8,128)S(1)} %get-tuple-element.57, f32[16,16,4096]{2,1,0:T(8,128)} %param.28, ...), kind=kLoop, calls=%fused_computation.25 | loop fusion | flops 7274496 | bytes 9701376 | tf_op jit(solution)/shard_map/reduce_sum | solution.py:56
  171.7 4.3 %gather_fusion.9 = f32[8,16,4096]{2,1,0:T(8,128)} fusion(f32[16,16,4096]{2,1,0:T(8,128)} %get-tuple-element.23, s32[1024]{0:T(1024)} %copy-done.28), kind=kCustom, calls=%fused_computation.9 | custom fusion | bytes 4194336 | tf_op jit(solution)/shard_map/gather | solution.py:126
  176.1 2.4 broadcast_in_dim.76
  178.5 4.3 %scatter_fusion.7 = f32[16,16,4096]{2,1,0:T(8,128)} fusion(f32[16,16,4096]{2,1,0:T(8,128)} %broadcast_in_dim.76, s32[8]{0:T(128)S(1)} %copy-done.26, f32[8,16,4096]{2,1,0:T(8,128)} %gather_fusion.9), kind=kCustom, calls=%fused_computation.18 | custom fusion | bytes 6291488 | tf_op jit(solution)/shard_map/scatter | solution.py:126
  182.7 56.6 %all-to-all-done.1 = bf16[16,256,512]{2,1,0:T(8,128)(2,1)} async-done(((bf16[16,256,512]{2,1,0:T(8,128)(2,1)}), bf16[16,256,512]{2,1,0:T(8,128)(2,1)}, u32[]{:S(2)}, u32[]{:S(2)}) %all-to-all-start.1) | async-done | bytes 4194336 | tf_op jit(solution)/shard_map/all_to_all | solution.py:142
  239.3 5.1 %all-to-all-start.3 = ((f32[16,16,4096]{2,1,0:T(8,128)}), f32[16,16,4096]{2,1,0:T(8,128)}, u32[]{:S(2)}, u32[]{:S(2)}) async-start(f32[16,16,4096]{2,1,0:T(8,128)} %scatter_fusion.7), calls=%async_computation.3 | async-start | bytes 8388608 | tf_op jit(solution)/shard_map/all_to_all | solution.py:133
  244.4 6.4 %copy.54 = bf16[16,256,512]{1,2,0:T(8,128)(2,1)} copy(bf16[16,256,512]{2,1,0:T(8,128)(2,1)} %scatter_fusion.1) | data formatting | bytes 8388608 | tf_op jit(solution)/shard_map/scatter | solution.py:107
  250.8 6.4 %copy.52 = bf16[16,256,512]{1,2,0:T(8,128)(2,1)} copy(bf16[16,256,512]{2,1,0:T(8,128)(2,1)} %scatter_fusion) | data formatting | bytes 8388608 | tf_op jit(solution)/shard_map/scatter | solution.py:101
  257.2 0.7 gather_fusion.2
  258.1 2.9 fusion.9
  261.0 0.7 copy-done.14
  262.0 4.2 %convolution_convert_fusion.1 = bf16[16,4,4,128]{3,2,1,0:T(4,128)(2,1)} fusion(bf16[16,256,4,128]{1,3,2,0:T(8,128)(2,1)} %bitcast.114, f32[16,4,4]{2,1,0:T(4,128)S(1)} %fusion.50, f32[16,4,4,256]{3,2,1,0:T(4,128)} %copy-done.14), kind=kOutput, calls=%fused_computation.44 | convolution fusion | flops 17007104 | bytes 4523008 | tf_op jit(solution)/shard_map/skgp,spkd->skgd/dot_general | solution.py:27
  266.3 0.9 stack_reshape.6
  267.2 1.6 fusion.12
  268.8 1.3 copy.63
  270.1 0.7 fusion.48
  270.8 1.2 fusion.52
  272.0 5.1 %gather_fusion.4 = bf16[16,256,512]{2,1,0:T(8,128)(2,1)} fusion(bf16[16,256,512]{2,1,0:T(8,128)(2,1)} %all-to-all-done, s32[1024]{0:T(1024)} %copy-done.27), kind=kCustom, calls=%fused_computation.4 | custom fusion | bytes 8388672 | tf_op jit(solution)/shard_map/gather | solution.py:129
  277.1 5.1 %gather_fusion.6 = bf16[16,256,512]{2,1,0:T(8,128)(2,1)} fusion(bf16[16,256,512]{2,1,0:T(8,128)(2,1)} %all-to-all-done.1, s32[1024]{0:T(1024)} %copy-done.27), kind=kCustom, calls=%fused_computation.6 | custom fusion | bytes 8388672 | tf_op jit(solution)/shard_map/gather | solution.py:129
  282.2 9.9 %broadcast_select_fusion.1 = (bf16[16,256,512]{2,1,0:T(8,128)(2,1)}, bf16[16,256,512]{2,1,0:T(8,128)(2,1)}) fusion(bf16[16,256,512]{2,1,0:T(8,128)(2,1)} %gather_fusion.4, bf16[16,256,512]{2,1,0:T(8,128)(2,1)} %scatter_fusion, pred[16]{0:T(512)(128)(4,1)S(1)} %copy-done.30, bf16[16,256,512]{2,1,0:T(8,128)(2,1)} %gather_fusion.6, ...), kind=kLoop, calls=%fused_computation.28 | loop fusion | flops 4194304 | bytes 25165840 | tf_op jit(solution)/shard_map/jit(_where)/select_n | solution.py:63
  292.1 2.6 scatter_fusion.5
  294.7 6.4 %copy.58 = bf16[16,256,512]{1,2,0:T(8,128)(2,1)} copy(bf16[16,256,512]{2,1,0:T(8,128)(2,1)} %scatter_fusion.5) | data formatting | bytes 8388608 | tf_op jit(solution)/shard_map/scatter | solution.py:149
  301.1 2.6 scatter_fusion.3
  303.7 6.3 %copy.56 = bf16[16,256,512]{1,2,0:T(8,128)(2,1)} copy(bf16[16,256,512]{2,1,0:T(8,128)(2,1)} %scatter_fusion.3) | data formatting | bytes 8388608 | tf_op jit(solution)/shard_map/scatter | solution.py:148
  310.1 2.8 fusion.7
  313.2 3.4 convolution_convert_fusion
  316.7 0.7 pad_maximum_fusion.3
  317.3 19.7 %all-to-all-done.3 = f32[16,16,4096]{2,1,0:T(8,128)} async-done(((f32[16,16,4096]{2,1,0:T(8,128)}), f32[16,16,4096]{2,1,0:T(8,128)}, u32[]{:S(2)}, u32[]{:S(2)}) %all-to-all-start.3) | async-done | bytes 4194336 | tf_op jit(solution)/shard_map/all_to_all | solution.py:133
  337.1 5.1 %gather_fusion.10 = f32[16,16,4096]{2,1,0:T(8,128)} fusion(f32[16,16,4096]{2,1,0:T(8,128)} %all-to-all-done.3, s32[1024]{0:T(1024)} %copy-done.27), kind=kCustom, calls=%fused_computation.10 | custom fusion | bytes 8388672 | tf_op jit(solution)/shard_map/gather | solution.py:129
  342.3 5.8 %multiply_reduce_fusion = (f32[16,4096]{1,0:T(8,128)S(1)}, f32[16,16,4096]{2,1,0:T(8,128)}) fusion(f32[16,16]{1,0:T(8,128)S(1)} %copy-done.23, f32[16,4096]{1,0:T(8,128)S(1)} %copy-done.12, f32[16,16]{1,0:T(8,128)S(1)} %copy-done.22, f32[16,4096]{1,0:T(8,128)S(1)} %get-tuple-element.59, f32[16,16,4096]{2,1,0:T(8,128)} %gather_fusion.10, ...), kind=kLoop, calls=%fused_computation.23 | loop fusion | flops 8323072 | bytes 13895696 | tf_op jit(solution)/shard_map/reduce_sum | solution.py:56
  348.5 0.7 pad_maximum_fusion.2
  (100 shorter events, 4.3 us)
Async XLA Ops:
  0.6 165.4 %copy-start = (bf16[256,4096]{1,0:T(8,128)(2,1)S(1)}, bf16[256,4096]{1,0:T(8,128)(2,1)}, u32[]{:S(2)}) copy-start(bf16[256,4096]{1,0:T(8,128)(2,1)} %param.35) | copy-start | bytes 6291460
  1.6 11.3 %copy-start.25 = (s32[8]{0:T(128)}, s32[8]{0:T(128)S(1)}, u32[]{:S(2)}) copy-start(s32[8]{0:T(128)S(1)} %get-tuple-element.53) | copy-start | bytes 100
  1.6 11.3 %copy-start.28 = (s32[1024]{0:T(1024)}, s32[1024]{0:T(1024)S(1)}, u32[]{:S(2)}) copy-start(s32[1024]{0:T(1024)S(1)} %pad_clamp_fusion.1) | copy-start | bytes 12292
  4.6 15.5 %copy-start.34 = (s32[16,2]{0,1:T(2,128)S(1)}, s32[16,2]{0,1:T(2,128)}, u32[]{:S(2)}) copy-start(s32[16,2]{0,1:T(2,128)} %param.21) | copy-start | bytes 388
  12.9 31.7 %all-to-all-start.2 = ((f32[16,3,4096]{2,1,0:T(4,128)}), f32[16,3,4096]{2,1,0:T(4,128)}, u32[]{:S(2)}, u32[]{:S(2)}) async-start(f32[16,3,4096]{2,1,0:T(4,128)} %scatter_fusion.6), calls=%async_computation.2 | async-start | bytes 2097152 | tf_op jit(solution)/shard_map/all_to_all | solution.py:132
  20.3 5.0 %copy-start.1 = (s32[256]{0:T(256)S(1)}, s32[256]{0:T(256)}, u32[]{:S(2)}) copy-start(s32[256]{0:T(256)} %param.20) | copy-start | bytes 3076
  29.8 6.8 %copy-start.26 = (s32[8]{0:T(128)S(1)}, s32[8]{0:T(128)}, u32[]{:S(2)}) copy-start(s32[8]{0:T(128)} %copy-done.25) | copy-start | bytes 100
  44.6 97.0 %all-to-all-start = ((bf16[16,256,512]{2,1,0:T(8,128)(2,1)}), bf16[16,256,512]{2,1,0:T(8,128)(2,1)}, u32[]{:S(2)}, u32[]{:S(2)}) async-start(bf16[16,256,512]{2,1,0:T(8,128)(2,1)} %scatter_fusion.2), calls=%async_computation | async-start | bytes 8388608 | tf_op jit(solution)/shard_map/all_to_all | solution.py:141
  71.8 76.6 %copy-start.31 = (s32[128,2]{0,1:T(2,128)S(1)}, s32[128,2]{0,1:T(2,128)}, u32[]{:S(2)}) copy-start(s32[128,2]{0,1:T(2,128)} %param.39) | copy-start | bytes 3076
  141.6 97.7 %all-to-all-start.1 = ((bf16[16,256,512]{2,1,0:T(8,128)(2,1)}), bf16[16,256,512]{2,1,0:T(8,128)(2,1)}, u32[]{:S(2)}, u32[]{:S(2)}) async-start(bf16[16,256,512]{2,1,0:T(8,128)(2,1)} %scatter_fusion.4), calls=%async_computation.1 | async-start | bytes 8388608 | tf_op jit(solution)/shard_map/all_to_all | solution.py:142
  148.7 10.4 %copy-start.29 = (pred[16]{0:T(512)(128)(4,1)}, pred[16]{0:T(512)(128)(4,1)S(1)}, u32[]{:S(2)}) copy-start(pred[16]{0:T(512)(128)(4,1)S(1)} %compare_reduce_fusion) | copy-start | bytes 52
  149.4 4.3 %copy-start.27 = (s32[1024]{0:T(1024)}, s32[1024]{0:T(1024)S(1)}, u32[]{:S(2)}) copy-start(s32[1024]{0:T(1024)S(1)} %pad_clamp_fusion) | copy-start | bytes 12292
  150.4 5.4 %copy-start.17 = (f32[4,4096]{1,0:T(4,128)S(1)}, f32[4,4096]{1,0:T(4,128)}, u32[]{:S(2)}) copy-start(f32[4,4096]{1,0:T(4,128)} %param.31) | copy-start | bytes 196612
  150.4 9.4 %copy-start.18 = (f32[4096]{0:T(1024)S(1)}, f32[4096]{0:T(1024)}, u32[]{:S(2)}) copy-start(f32[4096]{0:T(1024)} %param.32) | copy-start | bytes 49156
  153.7 6.9 %copy-start.11 = (bf16[4096,32]{0,1:T(8,128)(2,1)S(1)}, bf16[4096,32]{0,1:T(8,128)(2,1)}, u32[]{:S(2)}) copy-start(bf16[4096,32]{0,1:T(8,128)(2,1)} %param.34) | copy-start | bytes 786436
  153.7 7.3 %copy-start.4 = (bf16[4096,256]{1,0:T(8,128)(2,1)S(1)}, bf16[4096,256]{1,0:T(8,128)(2,1)}, u32[]{:S(2)}) copy-start(bf16[4096,256]{1,0:T(8,128)(2,1)} %param.33) | copy-start | bytes 6291460
  155.8 3.3 copy-start.2
  155.8 10.2 %copy-start.16 = (f32[4096]{0:T(1024)S(1)}, f32[4096]{0:T(1024)}, u32[]{:S(2)}) copy-start(f32[4096]{0:T(1024)} %param.36) | copy-start | bytes 49156
  159.1 0.7 copy-start.6
  159.1 1.5 copy-start.8
  160.7 5.8 %copy-start.5 = (f32[16,4096]{1,0:T(8,128)S(1)}, f32[16,4096]{1,0:T(8,128)}, u32[]{:S(2)}) copy-start(f32[16,4096]{1,0:T(8,128)} %exp.68) | copy-start | bytes 786436
  239.3 97.8 %all-to-all-start.3 = ((f32[16,16,4096]{2,1,0:T(8,128)}), f32[16,16,4096]{2,1,0:T(8,128)}, u32[]{:S(2)}, u32[]{:S(2)}) async-start(f32[16,16,4096]{2,1,0:T(8,128)} %scatter_fusion.7), calls=%async_computation.3 | async-start | bytes 8388608 | tf_op jit(solution)/shard_map/all_to_all | solution.py:133
  250.8 6.4 %copy-start.32 = (s32[16]{0:T(128)S(1)}, s32[16]{0:T(128)}, u32[]{:S(2)}) copy-start(s32[16]{0:T(128)} %get-tuple-element.30) | copy-start | bytes 196
  250.8 7.1 %copy-start.15 = (bf16[2,16,2048]{2,1,0:T(8,128)(2,1)S(1)}, bf16[2,16,2048]{2,1,0:T(8,128)(2,1)}, u32[]{:S(2)}) copy-start(bf16[2,16,2048]{2,1,0:T(8,128)(2,1)} %param.24) | copy-start | bytes 393220
  250.8 7.2 %copy-start.33 = (s32[16]{0:T(128)S(1)}, s32[16]{0:T(128)}, u32[]{:S(2)}) copy-start(s32[16]{0:T(128)} %get-tuple-element.33) | copy-start | bytes 196
  258.1 9.1 %copy-start.3 = (f32[16,3,4096]{2,1,0:T(4,128)S(1)}, f32[16,3,4096]{2,1,0:T(4,128)}, u32[]{:S(2)}) copy-start(f32[16,3,4096]{2,1,0:T(4,128)} %copy-done.2) | copy-start | bytes 2359300
  261.0 0.7 copy-start.14
  277.1 5.1 %copy-start.30 = (pred[16]{0:T(512)(128)(4,1)S(1)}, pred[16]{0:T(512)(128)(4,1)}, u32[]{:S(2)}) copy-start(pred[16]{0:T(512)(128)(4,1)} %copy-done.29) | copy-start | bytes 52
  282.2 9.9 %copy-start.21 = (bf16[16,512]{1,0:T(8,128)(2,1)S(1)}, bf16[16,512]{1,0:T(8,128)(2,1)}, u32[]{:S(2)}) copy-start(bf16[16,512]{1,0:T(8,128)(2,1)} %get-tuple-element.42) | copy-start | bytes 49156
  294.7 6.4 %copy-start.20 = (bf16[16,512]{1,0:T(8,128)(2,1)S(1)}, bf16[16,512]{1,0:T(8,128)(2,1)}, u32[]{:S(2)}) copy-start(bf16[16,512]{1,0:T(8,128)(2,1)} %get-tuple-element.40) | copy-start | bytes 49156
  317.3 24.9 %copy-start.12 = (f32[16,4096]{1,0:T(8,128)S(1)}, f32[16,4096]{1,0:T(8,128)}, u32[]{:S(2)}) copy-start(f32[16,4096]{1,0:T(8,128)} %get-tuple-element.26) | copy-start | bytes 786436
  317.3 24.9 %copy-start.22 = (f32[16,16]{1,0:T(8,128)S(1)}, f32[16,16]{1,0:T(8,128)}, u32[]{:S(2)}) copy-start(f32[16,16]{1,0:T(8,128)} %get-tuple-element.48) | copy-start | bytes 3076
  317.3 24.9 %copy-start.23 = (f32[16,16]{1,0:T(8,128)S(1)}, f32[16,16]{1,0:T(8,128)}, u32[]{:S(2)}) copy-start(f32[16,16]{1,0:T(8,128)} %get-tuple-element.49) | copy-start | bytes 3076
  342.2 5.9 %copy-start.7 = (f32[16,4096]{1,0:T(8,128)S(1)}, f32[16,4096]{1,0:T(8,128)}, u32[]{:S(2)}) copy-start(f32[16,4096]{1,0:T(8,128)} %copy-done.6) | copy-start | bytes 786436
  342.2 5.9 %copy-start.9 = (f32[16,4096]{1,0:T(8,128)S(1)}, f32[16,4096]{1,0:T(8,128)}, u32[]{:S(2)}) copy-start(f32[16,4096]{1,0:T(8,128)} %copy-done.8) | copy-start | bytes 786436
  342.2 5.9 %copy-start.10 = (f32[16,4096]{1,0:T(8,128)S(1)}, f32[16,4096]{1,0:T(8,128)}, u32[]{:S(2)}) copy-start(f32[16,4096]{1,0:T(8,128)} %get-tuple-element.22) | copy-start | bytes 786436
  342.3 5.9 %copy-start.13 = (bf16[2,16,4096]{2,1,0:T(8,128)(2,1)S(1)}, bf16[2,16,4096]{2,1,0:T(8,128)(2,1)}, u32[]{:S(2)}) copy-start(bf16[2,16,4096]{2,1,0:T(8,128)(2,1)} %param.30) | copy-start | bytes 786436
  342.3 5.9 %copy-start.19 = (f32[4096]{0:T(1024)S(1)}, f32[4096]{0:T(1024)}, u32[]{:S(2)}) copy-start(f32[4096]{0:T(1024)} %param.32) | copy-start | bytes 49156
  342.3 5.9 %copy-start.24 = (f32[4096]{0:T(1024)S(1)}, f32[4096]{0:T(1024)}, u32[]{:S(2)}) copy-start(f32[4096]{0:T(1024)} %param.38) | copy-start | bytes 49156
where the time goes:
time: 351 us; the launch traced here: 349 us
  waiting for transfers between devices  148 us (42%)
  local copies, waits for them, and re-layouts  121 us (34%)
  other arithmetic  35.5 us (10%)
  starting transfers between devices  23.3 us (7%)
  matrix products  16.2 us (5%)
  blocking collectives  4.08 us (1%)
    all_to_all x1, waiting for transfers between devices, shards(): lax.all_to_all(pack_moving(key_cache), 'replica', split_axis=0, concat_ax...  69.8 us
    all_to_all x1, waiting for transfers between devices, shards(): lax.all_to_all(pack_moving(value_cache), 'replica', split_axis=0, concat_...  56.6 us
    all_to_all x1, waiting for transfers between devices, shards(): lax.all_to_all(pack_moving(state_one), 'replica', split_axis=0, concat_ax...  19.7 us
    gather x4, local copies, waits for them, and re-layouts, take_arrived(): return keep_where(arrived, received[source_rep], local_rows)  18.7 us
    scatter x4, local copies, waits for them, and re-layouts, pack_moving(): return empty.at[leave_dest].set(local_rows[leave_slot])  18.5 us
    gather x4, local copies, waits for them, and re-layouts, pack_moving(): return empty.at[leave_dest].set(local_rows[leave_slot])  15.8 us
    select_n x2, other arithmetic, keep_where(): jnp.where(flags.reshape((flags.shape[0],) + (1,) * (staying.ndim - 1)), m...  11.9 us
    reduce_sum x2, other arithmetic, mamba_step(): jnp.sum(c_out[:, :, None] * state_new, axis=1) + skip_d * inputs_wide  11.1 us
  transfers between devices with their start and end apart: 4, of which 4 were waited for; matrix products, arithmetic and copies ran while one was open for 42% of the time, Pallas kernels for 0%

commit v1 on v0

v1 whole, which is shorter than its diff:
```python
import math

import jax
import jax.numpy as jnp
from jax import lax
from jax.sharding import PartitionSpec as P

HD = 128


def shards(
    lengths,
    page_table,
    key_pool,
    value_pool,
    queries,
    new_keys,
    new_values,
    conv_state,
    ssm_state,
    mamba_x,
    mamba_z,
    conv_weight,
    conv_bias,
    dt_down,
    bc_proj,
    dt_up,
    dt_bias,
    a_log,
    skip_d,
    moves,
):
    f32, bf16 = jnp.float32, jnp.bfloat16
    replica = lax.axis_index("replica")
    replicas = lax.axis_size("replica")
    slots = page_table.shape[0]
    span = page_table.shape[1] * key_pool.shape[1]
    width = key_pool.shape[2]
    kv_heads = width // HD
    group = queries.shape[2] // width
    channels = ssm_state.shape[2]
    states = ssm_state.shape[1]
    taps = conv_weight.shape[0]
    leaving = moves.shape[0] // replicas

    base = replica * slots
    mine = lax.dynamic_slice_in_dim(moves, replica * leaving, leaving, 0)
    leave_slot = mine[:, 0] - base
    shift = lax.rem(mine[:, 1] // slots - replica + replicas, replicas)
    from_rep = lax.rem(replica - shift + replicas, replicas)
    to_rep = mine[:, 1] // slots
    come = moves[from_rep * leaving + jnp.arange(leaving)]
    come_slot = come[:, 1] - base
    own_lengths = lax.dynamic_slice_in_dim(lengths, base, slots)
    lane_row = jnp.argmax(shift[None, :] == jnp.arange(1, replicas)[:, None], axis=1)

    scan_small = jnp.concatenate(
        [conv_state[leave_slot].astype(bf16), mamba_x[0][leave_slot][:, None]], axis=1
    ).reshape(leaving, taps * channels)
    asks = jnp.concatenate([queries[1], new_keys[1], new_values[1]], axis=1)
    forward = jnp.zeros((replicas, taps * channels), bf16).at[to_rep].set(scan_small)
    backward = jnp.zeros((replicas, asks.shape[1]), bf16).at[from_rep].set(asks[come_slot])
    small = lax.all_to_all(
        jnp.concatenate([forward, backward], axis=1),
        "replica",
        split_axis=0,
        concat_axis=0,
        tiled=True,
    )
    got_scan = small[from_rep, : taps * channels].reshape(leaving, taps, channels)
    got_asks = small[to_rep, taps * channels :]

    states16 = ssm_state.astype(bf16)
    lanes = []
    for k in range(1, replicas):
        block = states16[leave_slot[lane_row[k - 1]]]
        lanes.append(
            lax.ppermute(block, "replica", [(i, (i + k) % replicas) for i in range(replicas)])
        )

    asks_here = asks.at[leave_slot].set(got_asks)
    q2 = asks_here[:, : queries.shape[2]]
    k2 = asks_here[:, queries.shape[2] : queries.shape[2] + width]
    v2 = asks_here[:, queries.shape[2] + width :]
    slot_ids = jnp.arange(slots)
    heads = lambda t: t.reshape(t.shape[:-1] + (kv_heads, HD))
    keys = key_pool[page_table].reshape(slots, span, width)
    keys = keys.at[slot_ids, own_lengths].set(new_keys[0]).at[slot_ids, own_lengths + 1].set(k2)
    vals = value_pool[page_table].reshape(slots, span, width)
    vals = vals.at[slot_ids, own_lengths].set(new_values[0]).at[slot_ids, own_lengths + 1].set(v2)
    q = jnp.stack([queries[0], q2], axis=1).reshape(slots, 2, kv_heads, group, HD)
    scores = jnp.einsum("stkgd,spkd->sktgp", q, heads(keys), preferred_element_type=f32) * (
        1.0 / math.sqrt(HD)
    )
    last = own_lengths[:, None] + jnp.arange(2)[None]
    seen = jnp.arange(span)[None, None] <= last[:, :, None]
    scores = jnp.where(seen[:, None, :, None, :], scores, -1e30)
    expo = jnp.exp(scores - jnp.max(scores, axis=-1, keepdims=True))
    w = (expo / jnp.sum(expo, axis=-1, keepdims=True)).astype(bf16)
    att = jnp.einsum("sktgp,spkd->stkgd", w, heads(vals), preferred_element_type=f32)
    att = att.astype(bf16).reshape(slots, 2, queries.shape[2])
    back = jnp.zeros((replicas, queries.shape[2]), bf16).at[to_rep].set(att[leave_slot, 1])
    back = lax.all_to_all(back, "replica", split_axis=0, concat_axis=0, tiled=True)
    att_two = att[:, 1].at[come_slot].set(back[from_rep])

    proj = jnp.concatenate([dt_down, bc_proj], axis=1)
    rank = dt_down.shape[1]
    rate = jnp.exp(a_log)

    def front(win):
        xc = jax.nn.silu(jnp.sum(win * conv_weight[None], axis=1) + conv_bias).astype(bf16)
        both = lax.psum(jnp.dot(xc, proj, preferred_element_type=f32), "tensor")
        dt = jax.nn.softplus(
            jnp.dot(both[:, :rank].astype(bf16), dt_up, preferred_element_type=f32) + dt_bias
        )
        return xc.astype(f32), dt, both[:, rank : rank + states], both[:, rank + states :]

    def advance(h, xc, dt, b):
        return (
            jnp.exp(-dt[:, None, :] * rate[None]) * h
            + b[:, :, None] * (dt * xc)[:, None, :]
        )

    def emit(h, xc, c, z):
        out = jnp.sum(c[:, :, None] * h, axis=1) + skip_d * xc
        return (out * jax.nn.silu(z.astype(f32))).astype(bf16)

    win = jnp.concatenate([conv_state, mamba_x[0].astype(f32)[:, None]], axis=1)
    win = jnp.concatenate([win, got_scan.astype(f32)], axis=0)
    xc, dt, b, c = front(win)
    h_one = advance(ssm_state, xc[:slots], dt[:slots], b[:slots])
    mamba_one = emit(h_one, xc[:slots], c[:slots], mamba_z[0])

    win_two = win[:slots, 1:].at[come_slot].set(win[slots:, 1:])
    win_two = jnp.concatenate([win_two, mamba_x[1].astype(f32)[:, None]], axis=1)
    xc2, dt2, b2, c2 = front(win_two)

    got = jnp.stack(lanes)[shift - 1].astype(f32)
    h_got = advance(got, xc[slots:], dt[slots:], b[slots:])
    h_prev = h_one.at[come_slot].set(h_got)
    final_ssm = advance(h_prev, xc2, dt2, b2)
    mamba_two = emit(final_ssm, xc2, c2, mamba_z[1])
    return (
        jnp.stack([att[:, 0], att_two]),
        jnp.stack([mamba_one, mamba_two]),
        final_ssm,
        win_two[:, 1:],
    )


def solution(mesh):
    row, both = P("replica", None, "tensor"), P(None, "replica", "tensor")
    in_specs = (
        P(),
        P("replica", None),
        row,
        row,
        both,
        both,
        both,
        row,
        row,
        both,
        both,
        P(None, "tensor"),
        P("tensor"),
        P("tensor", None),
        P("tensor", None),
        P(None, "tensor"),
        P("tensor"),
        P(None, "tensor"),
        P("tensor"),
        P(),
    )
    return jax.shard_map(
        shards, mesh=mesh, in_specs=in_specs, out_specs=(both, both, row, row), check_vma=False
    )
```

time: 351 us -> 392 us (1.12)
  the two profiles are of different devices: /device:TPU:14 before, /device:TPU:0 now
where the time goes in v1:
time: 392 us; the launch traced here: 384 us
  local copies, waits for them, and re-layouts  171 us (44%)
  waiting for transfers between devices  66.1 us (17%)
  between operations  58.3 us (15%)
  other arithmetic  43.7 us (11%)
  starting transfers between devices  29.6 us (8%)
  matrix products  11.2 us (3%)
  blocking collectives  4.3 us (1%)
    gather x64, local copies, waits for them, and re-layouts  66.3 us
    ppermute x15, waiting for transfers between devices, shards(): lax.ppermute(block, 'replica', [(i, (i + k) % replicas) for i in range(re...  66.1 us
    unnamed x128, local copies, waits for them, and re-layouts  30.3 us
    ppermute x15, starting transfers between devices, shards(): lax.ppermute(block, 'replica', [(i, (i + k) % replicas) for i in range(re...  14.4 us
    reduce_sum x2, other arithmetic, emit(): out = jnp.sum(c[:, :, None] * h, axis=1) + skip_d * xc  12 us
    scatter x3, local copies, waits for them, and re-layouts, shards(): keys.at[slot_ids, own_lengths].set(new_keys[0])  11.6 us
    scatter x3, local copies, waits for them, and re-layouts, shards(): vals.at[slot_ids, own_lengths].set(new_values[0])  11.6 us
    all_to_all x1, starting transfers between devices, shards(): lax.all_to_all(jnp.concatenate([forward, backward], axis=1), 'replica', s...  8.36 us
  transfers between devices with their start and end apart: 17, of which 11 were waited for; matrix products, arithmetic and copies ran while one was open for 14% of the time, Pallas kernels for 0%

profile of v1, /device:TPU:0, one launch (start us, length us, event | category | flops | bytes accessed | tf_op | source)
XLA Modules:
  0.0 384.4 jit_solution(3866300077738194806)
XLA Ops:
  14.9 2.8 reduce.35
  17.7 2.4 reshape.494
  20.1 8.4 %all-to-all-start = ((bf16[16,2,9728]{2,1,0:T(2,128)(2,1)}), bf16[16,2,9728]{2,1,0:T(2,128)(2,1)}, u32[]{:S(2)}, u32[]{:S(2)}) async-start(bf16[16,2,9728]{2,1,0:T(2,128)(2,1)} %reshape.494), calls=%async_computation | async-start | bytes 1245184 | tf_op jit(solution)/shard_map/all_to_all | solution.py:63
  86.0 2.3 copy.112
  88.3 5.0 %gather_fusion.4 = bf16[32,128,512]{2,1,0:T(8,128)(2,1)} fusion(bf16[32,128,512]{2,1,0:T(8,128)(2,1)} %param.22, s32[1024]{0:T(1024)S(1)} %pad_clamp_fusion.5), kind=kCustom, calls=%fused_computation.5 | custom fusion | bytes 8388736 | tf_op jit(solution)/shard_map/gather | solution.py:87
  93.2 5.0 %gather_fusion = bf16[32,128,512]{2,1,0:T(8,128)(2,1)} fusion(bf16[32,128,512]{2,1,0:T(8,128)(2,1)} %param.23, s32[1024]{0:T(1024)S(1)} %pad_clamp_fusion.5), kind=kCustom, calls=%fused_computation | custom fusion | bytes 8388736 | tf_op jit(solution)/shard_map/gather | solution.py:89
  107.9 2.6 scatter_fusion.3
  110.5 2.6 scatter_fusion
  116.4 4.9 %reshape.495 = bf16[16,1,19456]{2,1,0:T(2,128)(2,1)} reshape(bf16[16,2,9728]{2,1,0:T(2,128)(2,1)} %all-to-all-done) | data formatting | bytes 1245184
  121.3 2.3 copy.135
  123.6 23.5 %while.2 = (s32[]{:T(128)}, bf16[16,19456]{1,0:T(8,128)(2,1)}, s32[8,2]{1,0:T(8,128)S(1)}, bf16[8,3072]{1,0:T(8,128)(2,1)S(1)}, s32[]{:T(128)}, /*index=5*/s32[]{:T(128)}) while((s32[]{:T(128)}, bf16[16,19456]{1,0:T(8,128)(2,1)}, s32[8,2]{1,0:T(8,128)S(1)}, bf16[8,3072]{1,0:T(8,128)(2,1)S(1)}, s32[]{:T(128)}, /*index=5*/s32[]{:T(128)}) %tuple.138), condition=%wide.while_cond, body=%wide.while_body.sunk | while | flops 2 | bytes 24697 | solution.py:71
  124.2 2.1 dynamic-slice.28
  127.1 2.1 dynamic-slice.28
  130.1 2.1 dynamic-slice.28
  133.0 2.1 dynamic-slice.28
  136.0 2.1 dynamic-slice.28
  138.9 2.1 dynamic-slice.28
  141.9 2.1 dynamic-slice.28
  144.8 2.1 dynamic-slice.28
  147.2 2.2 scatter_fusion.1
  152.1 43.0 %while.3 = (s32[]{:T(128)}, bf16[16,19456]{1,0:T(8,128)(2,1)}, s32[8,2]{1,0:T(8,128)}, bf16[8,16384]{1,0:T(8,128)(2,1)}, s32[]{:T(128)}, /*index=5*/s32[]{:T(128)}) while((s32[]{:T(128)}, bf16[16,19456]{1,0:T(8,128)(2,1)}, s32[8,2]{1,0:T(8,128)}, bf16[8,16384]{1,0:T(8,128)(2,1)}, s32[]{:T(128)}, /*index=5*/s32[]{:T(128)}) %tuple.137), condition=%wide.while_cond.1, body=%wide.while_body.1.sunk | while | flops 2 | bytes 131193 | solution.py:70
  153.4 2.2 dynamic-slice.30
  155.6 1.9 dynamic-update-slice.37
  158.8 2.2 dynamic-slice.30
  164.1 2.2 dynamic-slice.30
  166.4 1.9 dynamic-update-slice.37
  169.5 2.2 dynamic-slice.30
  174.9 2.2 dynamic-slice.30
  180.3 2.2 dynamic-slice.30
  185.6 2.2 dynamic-slice.30
  191.0 2.2 dynamic-slice.30
  195.2 2.2 reshape.305
  197.3 2.0 slice.254
  199.3 3.6 fusion.3
  204.8 2.2 fusion.9
  206.9 2.7 fusion.10
  210.9 4.3 %all-reduce.3 = (f32[24,288]{1,0:T(8,128)S(1)}, f32[16,288]{1,0:T(8,128)}) all-reduce(f32[24,288]{1,0:T(8,128)S(1)} %fusion.2, f32[16,288]{1,0:T(8,128)S(1)} %fusion.1), channel_id=1, replica_groups=mesh['replica'=16,'tensor'=2] {'tensor'}, use_global_device_ids=true, to_apply=%region_12.13 | all-reduce | flops 11520 | bytes 92160 | tf_op jit(solution)/shard_map/psum | solution.py:112
  218.6 2.6 scatter_fusion.4
  221.1 6.4 %copy.103 = bf16[16,256,512]{1,2,0:T(8,128)(2,1)} copy(bf16[16,256,512]{2,1,0:T(8,128)(2,1)} %scatter_fusion.4) | data formatting | bytes 8388608 | tf_op jit(solution)/shard_map/scatter | solution.py:88
  227.6 2.6 scatter_fusion.2
  230.2 6.4 %copy.102 = bf16[16,256,512]{1,2,0:T(8,128)(2,1)} copy(bf16[16,256,512]{2,1,0:T(8,128)(2,1)} %scatter_fusion.2) | data formatting | bytes 8388608 | tf_op jit(solution)/shard_map/scatter | solution.py:90
  236.6 3.9 %fusion.68 = (f32[16,4,2,4]{3,2,1,0:T(2,128)S(1)}, f32[16,4,2,4,256]{4,3,2,1,0:T(4,128)}) fusion(bf16[16,256,4,128,1]{1,3,4,2,0:T(8,128)(2,1)} %bitcast.214, pred[16,2,256]{2,1,0:T(4,128)(4,1)S(1)} %copy-done.24, bf16[16,1,4,4,128]{4,3,1,2,0:T(4,128)(2,1)S(1)} %stack.70, bf16[16,1,4,4,128]{4,3,1,2,0:T(4,128)(2,1)S(1)} %stack.69), kind=kOutput, calls=%fused_computation.229 | convolution fusion | flops 34341120 | bytes 4859904 | tf_op jit(solution)/shard_map/sub | solution.py:98
  240.5 3.6 fusion.7
  250.5 2.1 fusion.61
  255.8 6.9 %all-to-all-start.1 = ((bf16[16,2,1024]{2,1,0:T(2,128)(2,1)}), bf16[16,2,1024]{2,1,0:T(2,128)(2,1)S(1)}, u32[]{:S(2)}, u32[]{:S(2)}) async-start(bf16[16,2,1024]{2,1,0:T(2,128)(2,1)} %reshape.496), calls=%async_computation.1 | async-start | bytes 131072 | tf_op jit(solution)/shard_map/all_to_all | solution.py:103
  262.7 6.4 %multiply_reduce_fusion.1 = (f32[16,4096]{1,0:T(8,128)S(1)}, f32[16,16,4096]{2,1,0:T(8,128)}, bf16[16,16,4096]{2,1,0:T(8,128)(2,1)S(1)}) fusion(f32[16,16]{1,0:T(8,128)S(1)} %copy-done.39, f32[16,4096]{1,0:T(8,128)S(1)} %copy-done.14, f32[16,16]{1,0:T(8,128)S(1)} %copy-done.38, f32[16,16,4096]{2,1,0:T(8,128)} %param.28, f32[16,4096]{1,0:T(8,128)S(1)} %exp.50, ...), kind=kLoop, calls=%fused_computation.27 | loop fusion | flops 7274496 | bytes 11536384 | tf_op jit(solution)/shard_map/reduce_sum | solution.py:125
  270.2 5.5 %collective-permute-start.14 = (bf16[16,4096]{1,0:T(8,128)(2,1)S(1)}, bf16[16,4096]{1,0:T(8,128)(2,1)}, u32[]{:S(2)}, u32[]{:S(2)}) collective-permute-start(bf16[16,4096]{1,0:T(8,128)(2,1)S(1)} %get-tuple-element.129), channel_id=1, source_target_pairs={{0,30},{2,0},{4,2},{6,4},{8,6},{10,8},{12,10},{14,12},{16,14},{18,... | collective-permute-start | bytes 393224 | tf_op jit(solution)/shard_map/ppermute | solution.py:78
  277.4 2.4 collective-permute-start
  283.0 3.4 collective-permute-done
  289.3 5.0 %collective-permute-done.1 = bf16[16,4096]{1,0:T(8,128)(2,1)S(1)} collective-permute-done((bf16[16,4096]{1,0:T(8,128)(2,1)}, bf16[16,4096]{1,0:T(8,128)(2,1)S(1)}, u32[]{:S(2)}, u32[]{:S(2)}) %collective-permute-start.1) | collective-permute-done | bytes 131104 | tf_op jit(solution)/shard_map/ppermute | solution.py:78
  295.0 7.2 %collective-permute-done.2 = bf16[16,4096]{1,0:T(8,128)(2,1)S(1)} collective-permute-done((bf16[16,4096]{1,0:T(8,128)(2,1)}, bf16[16,4096]{1,0:T(8,128)(2,1)S(1)}, u32[]{:S(2)}, u32[]{:S(2)}) %collective-permute-start.2) | collective-permute-done | bytes 131104 | tf_op jit(solution)/shard_map/ppermute | solution.py:78
  302.9 6.3 %collective-permute-done.3 = bf16[16,4096]{1,0:T(8,128)(2,1)S(1)} collective-permute-done((bf16[16,4096]{1,0:T(8,128)(2,1)}, bf16[16,4096]{1,0:T(8,128)(2,1)S(1)}, u32[]{:S(2)}, u32[]{:S(2)}) %collective-permute-start.3) | collective-permute-done | bytes 131104 | tf_op jit(solution)/shard_map/ppermute | solution.py:78
  309.8 9.3 %collective-permute-done.4 = bf16[16,4096]{1,0:T(8,128)(2,1)S(1)} collective-permute-done((bf16[16,4096]{1,0:T(8,128)(2,1)}, bf16[16,4096]{1,0:T(8,128)(2,1)S(1)}, u32[]{:S(2)}, u32[]{:S(2)}) %collective-permute-start.4) | collective-permute-done | bytes 131104 | tf_op jit(solution)/shard_map/ppermute | solution.py:78
  319.7 6.9 %collective-permute-done.5 = bf16[16,4096]{1,0:T(8,128)(2,1)S(1)} collective-permute-done((bf16[16,4096]{1,0:T(8,128)(2,1)}, bf16[16,4096]{1,0:T(8,128)(2,1)S(1)}, u32[]{:S(2)}, u32[]{:S(2)}) %collective-permute-start.5) | collective-permute-done | bytes 131104 | tf_op jit(solution)/shard_map/ppermute | solution.py:78
  327.3 7.2 %collective-permute-done.6 = bf16[16,4096]{1,0:T(8,128)(2,1)S(1)} collective-permute-done((bf16[16,4096]{1,0:T(8,128)(2,1)}, bf16[16,4096]{1,0:T(8,128)(2,1)S(1)}, u32[]{:S(2)}, u32[]{:S(2)}) %collective-permute-start.6) | collective-permute-done | bytes 131104 | tf_op jit(solution)/shard_map/ppermute | solution.py:78
  335.2 7.7 %collective-permute-done.7 = bf16[16,4096]{1,0:T(8,128)(2,1)S(1)} collective-permute-done((bf16[16,4096]{1,0:T(8,128)(2,1)}, bf16[16,4096]{1,0:T(8,128)(2,1)S(1)}, u32[]{:S(2)}, u32[]{:S(2)}) %collective-permute-start.7) | collective-permute-done | bytes 131104 | tf_op jit(solution)/shard_map/ppermute | solution.py:78
  344.0 5.8 %collective-permute-done.8 = bf16[16,4096]{1,0:T(8,128)(2,1)S(1)} collective-permute-done((bf16[16,4096]{1,0:T(8,128)(2,1)S(1)}, bf16[16,4096]{1,0:T(8,128)(2,1)S(1)}, u32[]{:S(2)}, u32[]{:S(2)}) %collective-permute-start.8) | collective-permute-done | bytes 131104 | tf_op jit(solution)/shard_map/ppermute | solution.py:78
  351.3 4.3 %collective-permute-done.9 = bf16[16,4096]{1,0:T(8,128)(2,1)S(1)} collective-permute-done((bf16[16,4096]{1,0:T(8,128)(2,1)S(1)}, bf16[16,4096]{1,0:T(8,128)(2,1)S(1)}, u32[]{:S(2)}, u32[]{:S(2)}) %collective-permute-start.9) | collective-permute-done | bytes 131104 | tf_op jit(solution)/shard_map/ppermute | solution.py:78
  355.6 2.2 collective-permute-start.10
  358.5 3.0 collective-permute-done.10
  368.4 2.3 gather_fusion.5
  370.7 2.8 multiply_add_fusion.2
  373.5 4.2 %scatter_fusion.6 = f32[16,16,4096]{2,1,0:T(8,128)} fusion(f32[16,16,4096]{2,1,0:T(8,128)} %get-tuple-element.114, s32[8]{0:T(128)S(1)} %copy-done.45, f32[8,16,4096]{2,1,0:T(8,128)} %multiply_add_fusion.2), kind=kCustom, calls=%fused_computation.19 | custom fusion | bytes 6291488 | tf_op jit(solution)/shard_map/scatter | solution.py:140
  377.8 5.6 %multiply_reduce_fusion = (f32[16,4096]{1,0:T(8,128)S(1)}, f32[16,16,4096]{2,1,0:T(8,128)}) fusion(f32[16,16]{1,0:T(8,128)S(1)} %copy-done.35, f32[16,4096]{1,0:T(8,128)S(1)} %copy-done.19, f32[16,16]{1,0:T(8,128)S(1)} %copy-done.34, f32[16,16,4096]{2,1,0:T(8,128)} %scatter_fusion.6, f32[16,4096]{1,0:T(8,128)S(1)} %exp.50, f32[16,4096]{1,0:T(8,128)S(1)} %copy-done.18), kind=kLoop, calls=%fused_computation.25 | loop fusion | flops 6225920 | bytes 9439232 | tf_op jit(solution)/shard_map/reduce_sum | solution.py:125
  (256 shorter events, 97.6 us)
Async XLA Ops:
  0.6 215.8 %copy-start = (bf16[256,4096]{1,0:T(8,128)(2,1)S(1)}, bf16[256,4096]{1,0:T(8,128)(2,1)}, u32[]{:S(2)}) copy-start(bf16[256,4096]{1,0:T(8,128)(2,1)} %param.35) | copy-start | bytes 6291460
  0.6 5.8 %copy-start.1 = (f32[16,3,4096]{2,0,1:T(8,128)S(1)}, f32[16,3,4096]{2,0,1:T(8,128)}, u32[]{:S(2)}) copy-start(f32[16,3,4096]{2,0,1:T(8,128)} %param.27) | copy-start | bytes 2359300
  0.7 7.5 %copy-start.37 = (bf16[2,16,512]{2,1,0:T(8,128)(2,1)S(1)}, bf16[2,16,512]{2,1,0:T(8,128)(2,1)}, u32[]{:S(2)}) copy-start(bf16[2,16,512]{2,1,0:T(8,128)(2,1)} %param.26) | copy-start | bytes 98308
  0.7 7.5 %copy-start.36 = (bf16[2,16,512]{2,1,0:T(8,128)(2,1)S(1)}, bf16[2,16,512]{2,1,0:T(8,128)(2,1)}, u32[]{:S(2)}) copy-start(bf16[2,16,512]{2,1,0:T(8,128)(2,1)} %param.25) | copy-start | bytes 98308
  2.3 6.6 %copy-start.46 = (s32[8]{0:T(128)}, s32[8]{0:T(128)S(1)}, u32[]{:S(2)}) copy-start(s32[8]{0:T(128)S(1)} %get-tuple-element.185) | copy-start | bytes 100
  2.4 7.2 %copy-start.49 = (s32[8]{0:T(128)}, s32[8]{0:T(128)S(1)}, u32[]{:S(2)}) copy-start(s32[8]{0:T(128)S(1)} %get-tuple-element.91) | copy-start | bytes 100
  3.2 6.4 %copy-start.43 = (s32[8]{0:T(128)}, s32[8]{0:T(128)S(1)}, u32[]{:S(2)}) copy-start(s32[8]{0:T(128)S(1)} %fusion.41) | copy-start | bytes 100
  9.6 10.5 %copy-start.3 = (bf16[16,3072]{1,0:T(8,128)(2,1)}, bf16[16,3072]{1,0:T(8,128)(2,1)S(1)}, u32[]{:S(2)}) copy-start(bf16[16,3072]{1,0:T(8,128)(2,1)S(1)} %pad_maximum_fusion.8) | copy-start | bytes 294916
  14.3 14.1 %copy-start.50 = (s32[256]{0:T(256)S(1)}, s32[256]{0:T(256)}, u32[]{:S(2)}) copy-start(s32[256]{0:T(256)} %param.20) | copy-start | bytes 3076
  17.6 13.7 %copy-start.48 = (s32[16,2]{0,1:T(2,128)S(1)}, s32[16,2]{0,1:T(2,128)}, u32[]{:S(2)}) copy-start(s32[16,2]{0,1:T(2,128)} %param.21) | copy-start | bytes 388
  17.7 15.2 %copy-start.12 = (f32[16,1,4096]{2,0,1:T(8,128)S(1)}, f32[16,1,4096]{2,0,1:T(8,128)}, u32[]{:S(2)}) copy-start(f32[16,1,4096]{2,0,1:T(8,128)} %get-tuple-element.151) | copy-start | bytes 786436
  20.1 96.3 %all-to-all-start = ((bf16[16,2,9728]{2,1,0:T(2,128)(2,1)}), bf16[16,2,9728]{2,1,0:T(2,128)(2,1)}, u32[]{:S(2)}, u32[]{:S(2)}) async-start(bf16[16,2,9728]{2,1,0:T(2,128)(2,1)} %reshape.494), calls=%async_computation | async-start | bytes 1245184 | tf_op jit(solution)/shard_map/all_to_all | solution.py:63
  29.8 55.2 %copy-start.22 = (bf16[1,16,2048]{2,1,0:T(8,128)(2,1)S(1)}, bf16[1,16,2048]{2,1,0:T(8,128)(2,1)}, u32[]{:S(2)}) copy-start(bf16[1,16,2048]{2,1,0:T(8,128)(2,1)} %get-tuple-element.155) | copy-start | bytes 196612
  93.2 14.6 %copy-start.32 = (bf16[16,512]{1,0:T(8,128)(2,1)S(1)}, bf16[16,512]{1,0:T(8,128)(2,1)}, u32[]{:S(2)}) copy-start(bf16[16,512]{1,0:T(8,128)(2,1)} %get-tuple-element.161) | copy-start | bytes 49156
  93.2 17.2 %copy-start.31 = (bf16[16,512]{1,0:T(8,128)(2,1)S(1)}, bf16[16,512]{1,0:T(8,128)(2,1)}, u32[]{:S(2)}) copy-start(bf16[16,512]{1,0:T(8,128)(2,1)} %get-tuple-element.207) | copy-start | bytes 49156
  113.0 10.6 %copy-start.33 = (bf16[8,3072]{1,0:T(8,128)(2,1)S(1)}, bf16[8,3072]{1,0:T(8,128)(2,1)}, u32[]{:S(2)}) copy-start(bf16[8,3072]{1,0:T(8,128)(2,1)} %custom-call.27) | copy-start | bytes 147460
  116.3 30.8 %copy-start.47 = (s32[8]{0:T(128)S(1)}, s32[8]{0:T(128)}, u32[]{:S(2)}) copy-start(s32[8]{0:T(128)} %copy-done.46) | copy-start | bytes 100
  195.2 7.8 %copy-start.44 = (s32[8]{0:T(128)S(1)}, s32[8]{0:T(128)}, u32[]{:S(2)}) copy-start(s32[8]{0:T(128)} %copy-done.43) | copy-start | bytes 100
  199.3 5.4 %copy-start.20 = (f32[4,4096]{1,0:T(4,128)S(1)}, f32[4,4096]{1,0:T(4,128)}, u32[]{:S(2)}) copy-start(f32[4,4096]{1,0:T(4,128)} %param.31) | copy-start | bytes 196612
  204.7 4.9 %copy-start.7 = (f32[24,4096]{1,0:T(8,128)S(1)}, f32[24,4096]{1,0:T(8,128)}, u32[]{:S(2)}) copy-start(f32[24,4096]{1,0:T(8,128)} %fusion.3) | copy-start | bytes 1179652
  204.7 4.9 %copy-start.25 = (f32[4096]{0:T(1024)S(1)}, f32[4096]{0:T(1024)}, u32[]{:S(2)}) copy-start(f32[4096]{0:T(1024)} %param.32) | copy-start | bytes 49156
  204.7 5.0 %copy-start.11 = (bf16[4096,32]{1,0:T(8,128)(2,1)S(1)}, bf16[4096,32]{1,0:T(8,128)(2,1)}, u32[]{:S(2)}) copy-start(bf16[4096,32]{1,0:T(8,128)(2,1)} %copy.112) | copy-start | bytes 786436
  204.8 5.0 %copy-start.51 = (bf16[4096,256]{1,0:T(8,128)(2,1)S(1)}, bf16[4096,256]{1,0:T(8,128)(2,1)}, u32[]{:S(2)}) copy-start(bf16[4096,256]{1,0:T(8,128)(2,1)} %param.33) | copy-start | bytes 6291460
  209.8 7.9 %copy-start.4 = (f32[24,4096]{1,0:T(8,128)}, f32[24,4096]{1,0:T(8,128)S(1)}, u32[]{:S(2)}) copy-start(f32[24,4096]{1,0:T(8,128)S(1)} %fusion.57) | copy-start | bytes 1179652
  210.4 6.1 %copy-start.40 = (f32[4096]{0:T(1024)S(1)}, f32[4096]{0:T(1024)}, u32[]{:S(2)}) copy-start(f32[4096]{0:T(1024)} %param.36) | copy-start | bytes 49156
  210.9 7.6 %copy-start.21 = (bf16[16,2048]{1,0:T(8,128)(2,1)S(1)}, bf16[16,2048]{1,0:T(8,128)(2,1)}, u32[]{:S(2)}) copy-start(bf16[16,2048]{1,0:T(8,128)(2,1)} %slice.245) | copy-start | bytes 196612
  221.1 6.4 %copy-start.29 = (bf16[16,512]{1,0:T(8,128)(2,1)S(1)}, bf16[16,512]{1,0:T(8,128)(2,1)}, u32[]{:S(2)}) copy-start(bf16[16,512]{1,0:T(8,128)(2,1)} %get-tuple-element.158) | copy-start | bytes 49156
  230.2 6.4 %copy-start.24 = (pred[16,2,256]{2,1,0:T(4,128)(4,1)S(1)}, pred[16,2,256]{2,1,0:T(4,128)(4,1)}, u32[]{:S(2)}) copy-start(pred[16,2,256]{2,1,0:T(4,128)(4,1)} %iota_compare_fusion) | copy-start | bytes 24580
  240.5 8.6 %copy-start.2 = (f32[16,3,4096]{2,1,0:T(4,128)S(1)}, f32[16,3,4096]{2,1,0:T(4,128)}, u32[]{:S(2)}) copy-start(f32[16,3,4096]{2,1,0:T(4,128)} %fusion.10) | copy-start | bytes 2359300
  244.1 6.3 %copy-start.26 = (f32[4096]{0:T(1024)S(1)}, f32[4096]{0:T(1024)}, u32[]{:S(2)}) copy-start(f32[4096]{0:T(1024)} %param.32) | copy-start | bytes 49156
  250.5 12.2 %copy-start.13 = (f32[16,4096]{1,0:T(8,128)S(1)}, f32[16,4096]{1,0:T(8,128)}, u32[]{:S(2)}) copy-start(f32[16,4096]{1,0:T(8,128)} %get-tuple-element.146) | copy-start | bytes 786436
  250.5 12.2 %copy-start.14 = (f32[16,4096]{1,0:T(8,128)S(1)}, f32[16,4096]{1,0:T(8,128)}, u32[]{:S(2)}) copy-start(f32[16,4096]{1,0:T(8,128)} %get-tuple-element.147) | copy-start | bytes 786436
  250.5 12.2 %copy-start.38 = (f32[16,16]{1,0:T(8,128)S(1)}, f32[16,16]{1,0:T(8,128)}, u32[]{:S(2)}) copy-start(f32[16,16]{1,0:T(8,128)} %get-tuple-element.159) | copy-start | bytes 3076
  250.5 12.2 %copy-start.39 = (f32[16,16]{1,0:T(8,128)S(1)}, f32[16,16]{1,0:T(8,128)}, u32[]{:S(2)}) copy-start(f32[16,16]{1,0:T(8,128)} %get-tuple-element.160) | copy-start | bytes 3076
  255.8 25.4 %all-to-all-start.1 = ((bf16[16,2,1024]{2,1,0:T(2,128)(2,1)}), bf16[16,2,1024]{2,1,0:T(2,128)(2,1)S(1)}, u32[]{:S(2)}, u32[]{:S(2)}) async-start(bf16[16,2,1024]{2,1,0:T(2,128)(2,1)} %reshape.496), calls=%async_computation.1 | async-start | bytes 131072 | tf_op jit(solution)/shard_map/all_to_all | solution.py:103
  269.1 10.7 %copy-start.5 = (f32[24,4096]{1,0:T(8,128)S(1)}, f32[24,4096]{1,0:T(8,128)}, u32[]{:S(2)}) copy-start(f32[24,4096]{1,0:T(8,128)} %copy-done.4) | copy-start | bytes 1179652
  269.1 10.7 %copy-start.16 = (bf16[2,16,4096]{2,1,0:T(8,128)(2,1)S(1)}, bf16[2,16,4096]{2,1,0:T(8,128)(2,1)}, u32[]{:S(2)}) copy-start(bf16[2,16,4096]{2,1,0:T(8,128)(2,1)} %param.30) | copy-start | bytes 786436
  269.1 10.7 %copy-start.27 = (f32[4096]{0:T(1024)S(1)}, f32[4096]{0:T(1024)}, u32[]{:S(2)}) copy-start(f32[4096]{0:T(1024)} %param.38) | copy-start | bytes 49156
  269.1 11.4 %copy-start.42 = (f32[16,288]{1,0:T(8,128)S(1)}, f32[16,288]{1,0:T(8,128)}, u32[]{:S(2)}) copy-start(f32[16,288]{1,0:T(8,128)} %get-tuple-element.112) | copy-start | bytes 55300
  270.2 96.6 %collective-permute-start.14 = (bf16[16,4096]{1,0:T(8,128)(2,1)S(1)}, bf16[16,4096]{1,0:T(8,128)(2,1)}, u32[]{:S(2)}, u32[]{:S(2)}) collective-permute-start(bf16[16,4096]{1,0:T(8,128)(2,1)S(1)} %get-tuple-element.129), channel_id=1, source_target_pairs={{0,30},{2,0},{4,2},{6,4},{8,6},{10,8},{12,10},{14,12},{16,14},{18,... | collective-permute-start | bytes 393224 | tf_op jit(solution)/shard_map/ppermute | solution.py:78
  275.7 89.5 %collective-permute-start.13 = (bf16[16,4096]{1,0:T(8,128)(2,1)S(1)}, bf16[16,4096]{1,0:T(8,128)(2,1)}, u32[]{:S(2)}, u32[]{:S(2)}) collective-permute-start(bf16[16,4096]{1,0:T(8,128)(2,1)S(1)} %get-tuple-element.130), channel_id=1, source_target_pairs={{0,28},{2,30},{4,0},{6,2},{8,4},{10,6},{12,8},{14,10},{16,12},{18,... | collective-permute-start | bytes 393224 | tf_op jit(solution)/shard_map/ppermute | solution.py:78
  276.3 87.4 %collective-permute-start.12 = (bf16[16,4096]{1,0:T(8,128)(2,1)S(1)}, bf16[16,4096]{1,0:T(8,128)(2,1)}, u32[]{:S(2)}, u32[]{:S(2)}) collective-permute-start(bf16[16,4096]{1,0:T(8,128)(2,1)S(1)} %get-tuple-element.131), channel_id=1, source_target_pairs={{0,26},{2,28},{4,30},{6,0},{8,2},{10,4},{12,6},{14,8},{16,10},{18,... | collective-permute-start | bytes 393224 | tf_op jit(solution)/shard_map/ppermute | solution.py:78
  276.9 85.3 %collective-permute-start.11 = (bf16[16,4096]{1,0:T(8,128)(2,1)S(1)}, bf16[16,4096]{1,0:T(8,128)(2,1)}, u32[]{:S(2)}, u32[]{:S(2)}) collective-permute-start(bf16[16,4096]{1,0:T(8,128)(2,1)S(1)} %get-tuple-element.132), channel_id=1, source_target_pairs={{0,24},{2,26},{4,28},{6,30},{8,0},{10,2},{12,4},{14,6},{16,8},{18,... | collective-permute-start | bytes 393224 | tf_op jit(solution)/shard_map/ppermute | solution.py:78
  277.4 9.0 %collective-permute-start = (bf16[16,4096]{1,0:T(8,128)(2,1)}, bf16[16,4096]{1,0:T(8,128)(2,1)}, u32[]{:S(2)}, u32[]{:S(2)}) collective-permute-start(bf16[16,4096]{1,0:T(8,128)(2,1)} %get-tuple-element.143), channel_id=1, source_target_pairs={{0,2},{2,4},{4,6},{6,8},{8,10},{10,12},{12,14},{14,16},{16,18},{18... | collective-permute-start | bytes 393224 | tf_op jit(solution)/shard_map/ppermute | solution.py:78
  281.3 61.6 %copy-start.23 = (bf16[16,4096]{1,0:T(8,128)(2,1)S(1)}, bf16[16,4096]{1,0:T(8,128)(2,1)}, u32[]{:S(2)}) copy-start(bf16[16,4096]{1,0:T(8,128)(2,1)} %get-tuple-element.135) | copy-start | bytes 393220
  286.4 7.9 %collective-permute-start.1 = (bf16[16,4096]{1,0:T(8,128)(2,1)}, bf16[16,4096]{1,0:T(8,128)(2,1)S(1)}, u32[]{:S(2)}, u32[]{:S(2)}) collective-permute-start(bf16[16,4096]{1,0:T(8,128)(2,1)} %get-tuple-element.142), channel_id=1, source_target_pairs={{0,4},{2,6},{4,8},{6,10},{8,12},{10,14},{12,16},{14,18},{16,20},{1... | collective-permute-start | bytes 393224 | tf_op jit(solution)/shard_map/ppermute | solution.py:78
  294.3 7.9 %collective-permute-start.2 = (bf16[16,4096]{1,0:T(8,128)(2,1)}, bf16[16,4096]{1,0:T(8,128)(2,1)S(1)}, u32[]{:S(2)}, u32[]{:S(2)}) collective-permute-start(bf16[16,4096]{1,0:T(8,128)(2,1)} %get-tuple-element.141), channel_id=1, source_target_pairs={{0,6},{2,8},{4,10},{6,12},{8,14},{10,16},{12,18},{14,20},{16,22},{... | collective-permute-start | bytes 393224 | tf_op jit(solution)/shard_map/ppermute | solution.py:78
  302.2 7.0 %collective-permute-start.3 = (bf16[16,4096]{1,0:T(8,128)(2,1)}, bf16[16,4096]{1,0:T(8,128)(2,1)S(1)}, u32[]{:S(2)}, u32[]{:S(2)}) collective-permute-start(bf16[16,4096]{1,0:T(8,128)(2,1)} %get-tuple-element.140), channel_id=1, source_target_pairs={{0,8},{2,10},{4,12},{6,14},{8,16},{10,18},{12,20},{14,22},{16,24},... | collective-permute-start | bytes 393224 | tf_op jit(solution)/shard_map/ppermute | solution.py:78
  309.1 9.9 %collective-permute-start.4 = (bf16[16,4096]{1,0:T(8,128)(2,1)}, bf16[16,4096]{1,0:T(8,128)(2,1)S(1)}, u32[]{:S(2)}, u32[]{:S(2)}) collective-permute-start(bf16[16,4096]{1,0:T(8,128)(2,1)} %get-tuple-element.139), channel_id=1, source_target_pairs={{0,10},{2,12},{4,14},{6,16},{8,18},{10,20},{12,22},{14,24},{16,26}... | collective-permute-start | bytes 393224 | tf_op jit(solution)/shard_map/ppermute | solution.py:78
  319.1 7.6 %collective-permute-start.5 = (bf16[16,4096]{1,0:T(8,128)(2,1)}, bf16[16,4096]{1,0:T(8,128)(2,1)S(1)}, u32[]{:S(2)}, u32[]{:S(2)}) collective-permute-start(bf16[16,4096]{1,0:T(8,128)(2,1)} %get-tuple-element.138), channel_id=1, source_target_pairs={{0,12},{2,14},{4,16},{6,18},{8,20},{10,22},{12,24},{14,26},{16,28}... | collective-permute-start | bytes 393224 | tf_op jit(solution)/shard_map/ppermute | solution.py:78
  326.7 7.9 %collective-permute-start.6 = (bf16[16,4096]{1,0:T(8,128)(2,1)}, bf16[16,4096]{1,0:T(8,128)(2,1)S(1)}, u32[]{:S(2)}, u32[]{:S(2)}) collective-permute-start(bf16[16,4096]{1,0:T(8,128)(2,1)} %get-tuple-element.137), channel_id=1, source_target_pairs={{0,14},{2,16},{4,18},{6,20},{8,22},{10,24},{12,26},{14,28},{16,30}... | collective-permute-start | bytes 393224 | tf_op jit(solution)/shard_map/ppermute | solution.py:78
  334.6 8.4 %collective-permute-start.7 = (bf16[16,4096]{1,0:T(8,128)(2,1)}, bf16[16,4096]{1,0:T(8,128)(2,1)S(1)}, u32[]{:S(2)}, u32[]{:S(2)}) collective-permute-start(bf16[16,4096]{1,0:T(8,128)(2,1)} %get-tuple-element.136), channel_id=1, source_target_pairs={{0,16},{2,18},{4,20},{6,22},{8,24},{10,26},{12,28},{14,30},{16,0},... | collective-permute-start | bytes 393224 | tf_op jit(solution)/shard_map/ppermute | solution.py:78
  343.0 27.7 %copy-start.41 = (f32[8,16]{1,0:T(8,128)S(1)}, f32[8,16]{1,0:T(8,128)}, u32[]{:S(2)}) copy-start(f32[8,16]{1,0:T(8,128)} %slice.258) | copy-start | bytes 1540
  343.0 6.8 %collective-permute-start.8 = (bf16[16,4096]{1,0:T(8,128)(2,1)S(1)}, bf16[16,4096]{1,0:T(8,128)(2,1)S(1)}, u32[]{:S(2)}, u32[]{:S(2)}) collective-permute-start(bf16[16,4096]{1,0:T(8,128)(2,1)S(1)} %copy-done.23), channel_id=1, source_target_pairs={{0,18},{2,20},{4,22},{6,24},{8,26},{10,28},{12,30},{14,0},{16,2},{... | collective-permute-start | bytes 393224 | tf_op jit(solution)/shard_map/ppermute | solution.py:78
  349.7 5.9 %collective-permute-start.9 = (bf16[16,4096]{1,0:T(8,128)(2,1)S(1)}, bf16[16,4096]{1,0:T(8,128)(2,1)S(1)}, u32[]{:S(2)}, u32[]{:S(2)}) collective-permute-start(bf16[16,4096]{1,0:T(8,128)(2,1)S(1)} %get-tuple-element.134), channel_id=1, source_target_pairs={{0,20},{2,22},{4,24},{6,26},{8,28},{10,30},{12,0},{14,2},{16,4},{1... | collective-permute-start | bytes 393224 | tf_op jit(solution)/shard_map/ppermute | solution.py:78
  355.6 5.9 %collective-permute-start.10 = (bf16[16,4096]{1,0:T(8,128)(2,1)S(1)}, bf16[16,4096]{1,0:T(8,128)(2,1)S(1)}, u32[]{:S(2)}, u32[]{:S(2)}) collective-permute-start(bf16[16,4096]{1,0:T(8,128)(2,1)S(1)} %get-tuple-element.133), channel_id=1, source_target_pairs={{0,22},{2,24},{4,26},{6,28},{8,30},{10,0},{12,2},{14,4},{16,6},{18... | collective-permute-start | bytes 393224 | tf_op jit(solution)/shard_map/ppermute | solution.py:78
  373.5 4.3 %copy-start.18 = (f32[16,4096]{1,0:T(8,128)S(1)}, f32[16,4096]{1,0:T(8,128)}, u32[]{:S(2)}) copy-start(f32[16,4096]{1,0:T(8,128)} %get-tuple-element.148) | copy-start | bytes 786436
  373.5 4.3 %copy-start.19 = (f32[16,4096]{1,0:T(8,128)S(1)}, f32[16,4096]{1,0:T(8,128)}, u32[]{:S(2)}) copy-start(f32[16,4096]{1,0:T(8,128)} %get-tuple-element.149) | copy-start | bytes 786436
  373.5 4.3 %copy-start.34 = (f32[16,16]{1,0:T(8,128)S(1)}, f32[16,16]{1,0:T(8,128)}, u32[]{:S(2)}) copy-start(f32[16,16]{1,0:T(8,128)} %get-tuple-element.165) | copy-start | bytes 3076
  373.5 4.3 %copy-start.35 = (f32[16,16]{1,0:T(8,128)S(1)}, f32[16,16]{1,0:T(8,128)}, u32[]{:S(2)}) copy-start(f32[16,16]{1,0:T(8,128)} %get-tuple-element.166) | copy-start | bytes 3076
  377.8 5.7 %copy-start.10 = (f32[16,4096]{1,0:T(8,128)S(1)}, f32[16,4096]{1,0:T(8,128)}, u32[]{:S(2)}) copy-start(f32[16,4096]{1,0:T(8,128)} %copy-done.8) | copy-start | bytes 786436
  377.8 5.7 %copy-start.17 = (bf16[2,16,4096]{2,1,0:T(8,128)(2,1)S(1)}, bf16[2,16,4096]{2,1,0:T(8,128)(2,1)}, u32[]{:S(2)}) copy-start(bf16[2,16,4096]{2,1,0:T(8,128)(2,1)} %param.30) | copy-start | bytes 786436
  377.8 5.6 %copy-start.28 = (f32[4096]{0:T(1024)S(1)}, f32[4096]{0:T(1024)}, u32[]{:S(2)}) copy-start(f32[4096]{0:T(1024)} %param.38) | copy-start | bytes 49156
  377.8 5.8 %copy-start.15 = (bf16[1,16,4096]{2,1,0:T(8,128)(2,1)S(1)}, bf16[1,16,4096]{2,1,0:T(8,128)(2,1)}, u32[]{:S(2)}) copy-start(bf16[1,16,4096]{2,1,0:T(8,128)(2,1)} %fusion.28) | copy-start | bytes 393220
  (5 other events, 13.1 us)

commit v2 on v1

v2 whole, which is shorter than its diff:
```python
import functools
import math

import jax
import jax.numpy as jnp
from jax import lax
from jax.experimental import pallas as pl
from jax.experimental.pallas import tpu as pltpu
from jax.sharding import PartitionSpec as P

HD = 128
F32, BF16 = jnp.float32, jnp.bfloat16
MESH = pl.DeviceIdType.MESH
ANY = pl.BlockSpec(memory_space=pl.ANY)
VMEM = pl.BlockSpec(memory_space=pltpu.VMEM)
SMEM = pl.BlockSpec(memory_space=pltpu.SMEM)


def round_up(n, m):
    return (n + m - 1) // m * m


def silu(v):
    return v / (1.0 + jnp.exp(-v))


def softplus(v):
    return jnp.maximum(v, 0.0) + jnp.log1p(jnp.exp(-jnp.abs(v)))


def chunks(total):
    step = min(512, total)
    return [slice(i, i + step) for i in range(0, total, step)]


def exchange_kernel(
    sizes,
    moves,
    lengths,
    pages,
    keys_hbm,
    vals_hbm,
    asks,
    small,
    states_hbm,
    conv,
    mx,
    mz,
    conv_w,
    conv_b,
    down_hbm,
    bc_hbm,
    up_hbm,
    dt_b,
    a_log,
    skip,
    state_one,
    got_state,
    att,
    fconv,
    m_one,
    dt_moved,
    xc_moved,
    b_moved,
    dt_two,
    xc_two,
    b_two,
    c_two,
    table,
    keys,
    vals,
    h,
    down,
    bc_w,
    up,
    send_state,
    send_small,
    got_small,
    send_ask,
    got_ask,
    att_two,
    send_att,
    got_att,
    win,
    win_two,
    xc_all,
    dt_all,
    b_all,
    c_all,
    y,
    part,
    part_two,
    load_sem,
    state_s,
    state_r,
    small_s,
    small_r,
    ask_s,
    ask_r,
    att_s,
    att_r,
    part_s,
    part_r,
):
    R, T, S, L, H, KV = sizes
    C = small.shape[2] * 4
    N = a_log.shape[0]
    NR = win.shape[1]
    rank = down.shape[1]
    page = keys.shape[1]
    n_pages = pages.shape[1]
    me = lax.axis_index("replica")
    core = lax.axis_index("tensor")

    loads = [
        pltpu.make_async_copy(src, dst, load_sem.at[i])
        for i, (src, dst) in enumerate(
            [
                (states_hbm, h),
                (keys_hbm, keys),
                (vals_hbm, vals),
                (down_hbm, down),
                (bc_hbm, bc_w),
                (up_hbm, up),
            ]
        )
    ]
    for load in loads:
        load.start()

    barrier = pltpu.get_barrier_semaphore()

    def greet(k, _):
        pl.semaphore_signal(
            barrier, inc=1, device_id={"replica": lax.rem(me + k, R)}, device_id_type=MESH
        )
        return 0

    def greet_core(k, _):
        pl.semaphore_signal(
            barrier, inc=1, device_id={"tensor": lax.rem(core + k, T)}, device_id_type=MESH
        )
        return 0

    lax.fori_loop(1, R, greet, 0)
    lax.fori_loop(1, T, greet_core, 0)

    shift = [lax.div(moves[j, 1], S) for j in range(L)]
    out_slot = [lax.rem(moves[me * L + j, 0], S) for j in range(L)]
    lane_of = [jnp.maximum(shift[j] - 1, 0) for j in range(L)]
    in_slot = [
        lax.rem(moves[lax.rem(me - shift[j] + R, R) * L + j, 1], S) for j in range(L)
    ]

    def pick(values, k):
        found = values[0]
        for j in range(1, L):
            found = jnp.where(shift[j] == k, values[j], found)
        return found

    def source(g):
        row, lane = g, 0
        for j in range(L):
            hit = in_slot[j] == g
            row = jnp.where(hit, S + j, row)
            lane = jnp.where(hit, lane_of[j], lane)
        return row, lane

    def lane_copy(src, dst, send, recv, k, forward=True):
        to = lax.rem(me + k, R) if forward else lax.rem(me - k + R, R)
        return pltpu.make_async_remote_copy(
            src_ref=src.at[k - 1],
            dst_ref=dst.at[k - 1],
            send_sem=send.at[k - 1],
            recv_sem=recv.at[k - 1],
            device_id={"replica": to},
            device_id_type=MESH,
        )

    ask_copy = lambda k: lane_copy(send_ask, got_ask, ask_s, ask_r, k, False)
    small_copy = lambda k: lane_copy(send_small, got_small, small_s, small_r, k)
    state_copy = lambda k: lane_copy(send_state, got_state, state_s, state_r, k)
    att_copy = lambda k: lane_copy(send_att, got_att, att_s, att_r, k)

    pl.semaphore_wait(barrier, R - 1 + T - 1)

    def send_first(k, _):
        send_ask[k - 1] = asks[1, pick(in_slot, k)]
        ask_copy(k).start()
        send_small[k - 1] = small[pick(out_slot, k)]
        small_copy(k).start()
        return 0

    lax.fori_loop(1, R, send_first, 0)
    loads[0].wait()

    def send_states(k, _):
        slot = pick(out_slot, k)
        for c in chunks(C):
            send_state[k - 1, :, c] = h[slot, :, c].astype(BF16)
        state_copy(k).start()
        return 0

    lax.fori_loop(1, R, send_states, 0)

    for g in range(S):
        row, lane = source(g)
        table[g] = row
        table[S + g] = lane

    loads[1].wait()
    loads[2].wait()
    lax.fori_loop(1, R, lambda k, _: (ask_copy(k).wait(), 0)[1], 0)

    rows = 2 * H
    head_of = lax.broadcasted_iota(jnp.int32, (rows, 1), 0) % H // (H // KV)
    step_of = lax.broadcasted_iota(jnp.int32, (rows, 1), 0) // H
    ask_col = lax.broadcasted_iota(jnp.int32, (rows, asks.shape[2]), 1)
    pos = lax.broadcasted_iota(jnp.int32, (rows, n_pages * page), 1)
    is_key = ask_col == H + head_of
    is_val = ask_col == H + KV + head_of
    nt = (((1,), (1,)), ((), ()))
    nn = (((1,), (0,)), ((), ()))

    def attend(g, _):
        length = lengths[me * S + g]
        gone = jnp.int32(0)
        lane = jnp.int32(0)
        for j in range(L):
            hit = out_slot[j] == g
            gone = jnp.where(hit, 1, gone)
            lane = jnp.where(hit, lane_of[j], lane)
        one = asks[0, g]
        two = jnp.where(gone == 1, got_ask[lane].astype(F32), asks[1, g].astype(F32)).astype(BF16)
        q = jnp.concatenate([one.astype(F32)[:H], two.astype(F32)[:H]], axis=0)
        qb = q.astype(BF16)
        wide = jnp.concatenate(
            [jnp.where(head_of == i, q, 0.0) for i in range(KV)], axis=1
        ).astype(BF16)
        scores = jnp.concatenate(
            [
                lax.dot_general(wide, keys[pages[g, p]], nt, preferred_element_type=F32)
                for p in range(n_pages)
            ],
            axis=1,
        )
        new_one = lax.dot_general(qb, one, nt, preferred_element_type=F32)
        new_two = lax.dot_general(qb, two, nt, preferred_element_type=F32)
        new_one = jnp.sum(jnp.where(is_key, new_one, 0.0), axis=1, keepdims=True)
        new_two = jnp.sum(jnp.where(is_key, new_two, 0.0), axis=1, keepdims=True)
        at_one, at_two = pos == length, pos == length + 1
        scores = jnp.where(at_one, new_one, jnp.where(at_two, new_two, scores))
        scores = scores * (1.0 / math.sqrt(HD))
        scores = jnp.where(pos <= length + step_of, scores, -1e30)
        expo = jnp.exp(scores - jnp.max(scores, axis=1, keepdims=True))
        w = expo / jnp.sum(expo, axis=1, keepdims=True)
        w_one = jnp.sum(jnp.where(at_one, w, 0.0), axis=1, keepdims=True)
        w_two = jnp.sum(jnp.where(at_two, w, 0.0), axis=1, keepdims=True)
        w = jnp.where(at_one | at_two, 0.0, w).astype(BF16)
        mixed = lax.dot_general(
            w[:, :page], vals[pages[g, 0]], nn, preferred_element_type=F32
        )
        for p in range(1, n_pages):
            mixed += lax.dot_general(
                w[:, p * page : (p + 1) * page],
                vals[pages[g, p]],
                nn,
                preferred_element_type=F32,
            )
        out = lax.dot_general(
            jnp.where(is_val, w_one, 0.0).astype(BF16), one, nn, preferred_element_type=F32
        ) + lax.dot_general(
            jnp.where(is_val, w_two, 0.0).astype(BF16), two, nn, preferred_element_type=F32
        )
        for i in range(KV):
            out += jnp.where(head_of == i, mixed[:, i * HD : (i + 1) * HD], 0.0)
        first, second = out[:H], out[H:]
        if att.shape[2] > H:
            pad = jnp.zeros((att.shape[2] - H, HD), F32)
            first = jnp.concatenate([first, pad], axis=0)
            second = jnp.concatenate([second, pad], axis=0)
        att[0, g] = first.astype(BF16)
        att_two[g] = second.astype(BF16)
        return 0

    lax.fori_loop(0, S, attend, 0, unroll=2)

    def send_back(k, _):
        send_att[k - 1] = att_two[pick(out_slot, k)]
        att_copy(k).start()
        return 0

    lax.fori_loop(1, R, send_back, 0)

    for k in range(3):
        win[k, :S] = conv[k]
    win[3, :S] = mx[0].astype(F32)
    lax.fori_loop(1, R, lambda k, _: (small_copy(k).wait(), 0)[1], 0)
    for j in range(L):
        tile = got_small[lane_of[j]].astype(F32)
        for k in range(4):
            win[k, S + j : S + j + 1] = jnp.concatenate(
                [tile[4 * k + i : 4 * k + i + 1] for i in range(4)], axis=1
            )
    for k in range(4):
        win[k, S + L :] = jnp.zeros((NR - S - L, C), F32)

    def project(src, n, xc_ref, buf):
        low = jnp.zeros((n, rank), F32)
        bc = jnp.zeros((n, bc_w.shape[1]), F32)
        for c in chunks(C):
            total = conv_b[:, c] + src(0, c) * conv_w[0:1, c]
            for k in range(1, 4):
                total += src(k, c) * conv_w[k : k + 1, c]
            xb = silu(total).astype(BF16)
            xc_ref[:, c] = xb.astype(F32)
            low += lax.dot_general(xb, down[c], nn, preferred_element_type=F32)
            bc += lax.dot_general(xb, bc_w[c], nn, preferred_element_type=F32)
        buf[core, :, :rank] = low
        buf[core, :, rank:] = jnp.concatenate(
            [bc, jnp.zeros((n, HD - bc.shape[1]), F32)], axis=1
        )

    def core_copy(buf, which, k):
        return pltpu.make_async_remote_copy(
            src_ref=buf.at[core],
            dst_ref=buf.at[core],
            send_sem=part_s.at[which, k],
            recv_sem=part_r.at[which, k],
            device_id={"tensor": lax.rem(core + k, T)},
            device_id_type=MESH,
        )

    def reduce_parts(buf, which):
        lax.fori_loop(1, T, lambda k, _: (core_copy(buf, which, k).start(), 0)[1], 0)
        lax.fori_loop(1, T, lambda k, _: (core_copy(buf, which, k).wait(), 0)[1], 0)
        total = buf[0]
        for t in range(1, T):
            total += buf[t]
        return total

    def steps(total, n, dt_ref, b_ref, c_ref):
        low = total[:, :rank].astype(BF16)
        for c in chunks(C):
            dt_ref[:, c] = softplus(
                lax.dot_general(low, up[:, c], nn, preferred_element_type=F32) + dt_b[:, c]
            )
        turned = total[:, rank : rank + HD].T
        for i in range(n):
            b_ref[i] = jnp.broadcast_to(turned[:N, i : i + 1], (N, HD))
            c_ref[i] = jnp.broadcast_to(turned[N : 2 * N, i : i + 1], (N, HD))

    loads[3].wait()
    loads[4].wait()
    loads[5].wait()
    project(lambda k, c: win[k, :, c], NR, xc_all, part)
    steps(reduce_parts(part, 0), NR, dt_all, b_all, c_all)
    dt_moved[...] = dt_all[S:]
    xc_moved[...] = xc_all[S:]
    b_moved[...] = b_all[S:]

    for g in range(S):
        row, _ = source(g)
        for k in range(3):
            win_two[k, g : g + 1] = win[k + 1, pl.ds(row, 1), :]
    win_two[3] = mx[1].astype(F32)
    for k in range(3):
        fconv[k] = win_two[k + 1]
    project(lambda k, c: win_two[k, :, c], S, xc_two, part_two)
    steps(reduce_parts(part_two, 1), S, dt_two, b_two, c_two)

    def scan(g, _):
        reps = 512 // HD if C >= 512 else C // HD
        b = jnp.concatenate([b_all[g]] * reps, axis=1)
        cc = jnp.concatenate([c_all[g]] * reps, axis=1)
        for c in chunks(C):
            dt = dt_all[pl.ds(g, 1), c]
            x = xc_all[pl.ds(g, 1), c]
            new = jnp.exp(-dt * jnp.exp(a_log[:, c])) * h[g, :, c] + b * (dt * x)
            h[g, :, c] = new
            y[pl.ds(g, 1), c] = jnp.sum(cc * new, axis=0, keepdims=True)
        return 0

    lax.fori_loop(0, S, scan, 0)
    save = pltpu.make_async_copy(h, state_one, load_sem.at[0])
    save.start()
    for c in chunks(C):
        m_one[:, c] = (
            (y[:, c] + skip[:, c] * xc_all[:S, c]) * silu(mz[0, :, c].astype(F32))
        ).astype(BF16)

    lax.fori_loop(1, R, lambda k, _: (att_copy(k).wait(), 0)[1], 0)
    for g in range(S):
        row, lane = source(g)
        att[1, g] = jnp.where(
            row >= S, got_att[lane].astype(F32), att_two[g].astype(F32)
        ).astype(BF16)
    save.wait()
    lax.fori_loop(1, R, lambda k, _: (state_copy(k).wait(), 0)[1], 0)


def finish_kernel(
    sizes,
    table,
    kept,
    arrived,
    dt_moved,
    xc_moved,
    b_moved,
    dt_two,
    xc_two,
    b_two,
    c_two,
    a_log,
    skip,
    mz,
    m_one,
    final,
    out,
    rate,
    y,
):
    S = sizes
    C = final.shape[2]
    g = pl.program_id(0)
    row = table[g]
    reps = min(512, C) // HD

    @pl.when(g == 0)
    def _():
        rate[...] = jnp.exp(a_log[...])
        out[0] = m_one[...]

    wide = lambda v: jnp.concatenate([v] * reps, axis=1)

    def second(prev, c):
        dt, x = dt_two[pl.ds(g, 1), c], xc_two[pl.ds(g, 1), c]
        new = jnp.exp(-dt * rate[:, c]) * prev + wide(b_two[g]) * (dt * x)
        final[0, :, c] = new
        y[pl.ds(g, 1), c] = jnp.sum(wide(c_two[g]) * new, axis=0, keepdims=True)

    @pl.when(row < S)
    def _():
        for c in chunks(C):
            second(kept[0, :, c], c)

    @pl.when(row >= S)
    def _():
        j = row - S
        for c in chunks(C):
            dt, x = dt_moved[pl.ds(j, 1), c], xc_moved[pl.ds(j, 1), c]
            one = jnp.exp(-dt * rate[:, c]) * arrived[0, :, c].astype(F32)
            second(one + wide(b_moved[j]) * (dt * x), c)

    @pl.when(g == S - 1)
    def _():
        for c in chunks(C):
            out[1, :, c] = (
                (y[:, c] + skip[:, c] * xc_two[:, c]) * silu(mz[1, :, c].astype(F32))
            ).astype(BF16)


def shards(
    lengths,
    page_table,
    key_pool,
    value_pool,
    queries,
    new_keys,
    new_values,
    conv_state,
    ssm_state,
    mamba_x,
    mamba_z,
    conv_weight,
    conv_bias,
    dt_down,
    bc_proj,
    dt_up,
    dt_bias,
    a_log,
    skip_d,
    moves,
):
    R, T = lax.axis_size("replica"), lax.axis_size("tensor")
    S, N, C = ssm_state.shape
    L = moves.shape[0] // R
    QW, W = queries.shape[2], key_pool.shape[2]
    H, KV = QW // HD, W // HD
    A = round_up(H + 2 * KV, 16)
    AH = round_up(H, 16)
    NR = S + round_up(L, 16)
    rank = dt_down.shape[1]

    heads = lambda t: t.reshape(2, S, -1, HD)
    asks = jnp.concatenate(
        [
            heads(queries),
            heads(new_keys),
            heads(new_values),
            jnp.zeros((2, S, A - H - 2 * KV, HD), BF16),
        ],
        axis=2,
    )
    small = jnp.concatenate(
        [conv_state.astype(BF16), mamba_x[0][:, None]], axis=1
    ).reshape(S, 16, C // 4)
    conv = jnp.transpose(conv_state, (1, 0, 2))
    row = lambda v: v.reshape(1, C)
    shape = jax.ShapeDtypeStruct
    dma = pltpu.SemaphoreType.DMA
    outs = pl.pallas_call(
        functools.partial(exchange_kernel, (R, T, S, L, H, KV)),
        out_shape=(
            shape((S, N, C), F32),
            shape((R - 1, N, C), BF16),
            shape((2, S, AH, HD), BF16),
            shape((3, S, C), F32),
            shape((S, C), BF16),
            shape((NR - S, C), F32),
            shape((NR - S, C), F32),
            shape((NR - S, N, HD), F32),
            shape((S, C), F32),
            shape((S, C), F32),
            shape((S, N, HD), F32),
            shape((S, N, HD), F32),
            shape((2 * S,), jnp.int32),
        ),
        in_specs=[SMEM, SMEM, SMEM, ANY, ANY, VMEM, VMEM, ANY]
        + [VMEM] * 5
        + [ANY] * 3
        + [VMEM] * 3,
        out_specs=(ANY, ANY) + (VMEM,) * 10 + (SMEM,),
        scratch_shapes=[
            pltpu.VMEM(key_pool.shape, BF16),
            pltpu.VMEM(value_pool.shape, BF16),
            pltpu.VMEM((S, N, C), F32),
            pltpu.VMEM(dt_down.shape, BF16),
            pltpu.VMEM(bc_proj.shape, BF16),
            pltpu.VMEM(dt_up.shape, BF16),
            pltpu.VMEM((R - 1, N, C), BF16),
            pltpu.VMEM((R - 1, 16, C // 4), BF16),
            pltpu.VMEM((R - 1, 16, C // 4), BF16),
            pltpu.VMEM((R - 1, A, HD), BF16),
            pltpu.VMEM((R - 1, A, HD), BF16),
            pltpu.VMEM((S, AH, HD), BF16),
            pltpu.VMEM((R - 1, AH, HD), BF16),
            pltpu.VMEM((R - 1, AH, HD), BF16),
            pltpu.VMEM((4, NR, C), F32),
            pltpu.VMEM((4, S, C), F32),
            pltpu.VMEM((NR, C), F32),
            pltpu.VMEM((NR, C), F32),
            pltpu.VMEM((NR, N, HD), F32),
            pltpu.VMEM((NR, N, HD), F32),
            pltpu.VMEM((S, C), F32),
            pltpu.VMEM((T, NR, rank + HD), F32),
            pltpu.VMEM((T, S, rank + HD), F32),
            dma((6,)),
        ]
        + [dma((R - 1,))] * 8
        + [dma((2, T))] * 2,
        compiler_params=pltpu.CompilerParams(
            collective_id=0, has_side_effects=True, vmem_limit_bytes=48 * 1024 * 1024
        ),
        name="exchange",
    )(
        moves,
        lengths,
        page_table,
        key_pool,
        value_pool,
        asks,
        small,
        ssm_state,
        conv,
        mamba_x,
        mamba_z,
        conv_weight,
        row(conv_bias),
        dt_down,
        bc_proj,
        dt_up,
        row(dt_bias),
        a_log,
        row(skip_d),
    )
    state_one, got_state, att, fconv, m_one = outs[:5]
    table = outs[12]
    whole = lambda v: pl.BlockSpec(v.shape, lambda g, t: (0,) * v.ndim)
    rest = list(outs[5:12]) + [a_log, row(skip_d), mamba_z, m_one]
    final_ssm, mamba_out = pl.pallas_call(
        functools.partial(finish_kernel, S),
        grid_spec=pltpu.PrefetchScalarGridSpec(
            num_scalar_prefetch=1,
            grid=(S,),
            in_specs=[
                pl.BlockSpec((1, N, C), lambda g, t: (g, 0, 0)),
                pl.BlockSpec((1, N, C), lambda g, t: (t[S + g], 0, 0)),
            ]
            + [whole(v) for v in rest],
            out_specs=[
                pl.BlockSpec((1, N, C), lambda g, t: (g, 0, 0)),
                pl.BlockSpec((2, S, C), lambda g, t: (0, 0, 0)),
            ],
            scratch_shapes=[pltpu.VMEM((N, C), F32), pltpu.VMEM((S, C), F32)],
        ),
        out_shape=(shape((S, N, C), F32), shape((2, S, C), BF16)),
        compiler_params=pltpu.CompilerParams(vmem_limit_bytes=32 * 1024 * 1024),
        name="finish",
    )(table, state_one, got_state, *rest)
    return (
        att[:, :, :H].reshape(2, S, QW),
        mamba_out,
        final_ssm,
        jnp.transpose(fconv, (1, 0, 2)),
    )


def solution(mesh):
    row, both = P("replica", None, "tensor"), P(None, "replica", "tensor")
    in_specs = (
        P(),
        P("replica", None),
        row,
        row,
        both,
        both,
        both,
        row,
        row,
        both,
        both,
        P(None, "tensor"),
        P("tensor"),
        P("tensor", None),
        P("tensor", None),
        P(None, "tensor"),
        P("tensor"),
        P(None, "tensor"),
        P("tensor"),
        P(),
    )
    return jax.shard_map(
        shards, mesh=mesh, in_specs=in_specs, out_specs=(both, both, row, row), check_vma=False
    )
```

time: 392 us -> 120 us (0.31); the launches traced: 384 us -> 119 us
  local copies, waits for them, and re-layouts: 171 us -> 32.5 us
  Pallas kernels: 0 us -> 84.8 us
  waiting for transfers between devices: 66.1 us -> 0 us
  between operations: 58.3 us -> 0.83 us
  other arithmetic: 43.7 us -> 1.34 us
  starting transfers between devices: 29.6 us -> 0 us
  matrix products: 11.2 us -> 0 us
  blocking collectives: 4.3 us -> 0 us
    pallas_call x0 -> x2, Pallas kernels: none -> 84.8 us  [the longest x1 76.8 us: shards(): pl.pallas_call(functools.partial(exchange_kernel, (R, T, S, L, H, KV)), o...]
    gather x70 -> x0, local copies, waits for them, and re-layouts: 80.8 us -> none
    ppermute x15 -> x0, waiting for transfers between devices: 66.1 us -> none  [shards(): lax.ppermute(block, 'replica', [(i, (i + k) % replicas) for i in range(re...]
    scatter x13 -> x0, local copies, waits for them, and re-layouts: 37.1 us -> none  [the longest x3 11.6 us: shards(): keys.at[slot_ids, own_lengths].set(new_keys[0])]
    reduce_sum x4 -> x0, other arithmetic: 17.8 us -> none  [the longest x2 12 us: emit(): out = jnp.sum(c[:, :, None] * h, axis=1) + skip_d * xc]
    all_to_all x2 -> x0, starting transfers between devices: 15.2 us -> none  [the longest x1 8.36 us: shards(): lax.all_to_all(jnp.concatenate([forward, backward], axis=1), 'replica', s...]
    ppermute x15 -> x0, starting transfers between devices: 14.4 us -> none  [shards(): lax.ppermute(block, 'replica', [(i, (i + k) % replicas) for i in range(re...]
    slice x8 -> x0, local copies, waits for them, and re-layouts: 8.93 us -> none  [the longest x1 1.97 us: shards(): win_two = win[:slots, 1:].at[come_slot].set(win[slots:, 1:])]
  transfers between devices with their start and end apart: 17 -> 0, of which waited for: 11 -> 0; matrix products, arithmetic and copies ran while one was open for 14% -> 0% of each run, Pallas kernels for 0% -> 0%
where the time goes in v2:
time: 120 us; the launch traced here: 119 us
  Pallas kernels  84.8 us (71%)
  local copies, waits for them, and re-layouts  32.5 us (27%)
  other arithmetic  1.34 us (1%)
    pallas_call x1, Pallas kernels, shards(): pl.pallas_call(functools.partial(exchange_kernel, (R, T, S, L, H, KV)), o...  76.8 us
    unnamed x71, local copies, waits for them, and re-layouts  27.6 us
    pallas_call x1, Pallas kernels, shards(): pl.pallas_call(functools.partial(finish_kernel, S), grid_spec=pltpu.Prefe...  7.99 us

profile of v2, /device:TPU:0, one launch (start us, length us, event | category | flops | bytes accessed | tf_op | source)
XLA Modules:
  0.0 119.5 jit_solution(16927909980734961148)
XLA Ops:
  0.6 0.0 copy-start.4
  0.6 0.0 copy-start.3
  0.7 0.0 copy-start.7
  0.7 0.0 copy-start.1
  0.7 0.0 copy-start.26
  0.7 0.0 copy-start.25
  0.7 0.1 pad.5.clone
  0.8 1.4 %copy.26.pages = s32[16,2]{1,0:T(8,128)} copy(s32[16,2]{0,1:T(2,128)} %param.21) | data formatting | bytes 256 | tf_op args[1]
  2.2 0.8 reshape.34
  3.0 0.8 reshape.35
  3.8 0.8 copy.25.moves
  4.6 0.9 copy.28
  5.5 0.1 maximum_maximum_fusion.asks
  5.6 0.9 slice_bitcast_fusion
  6.5 1.2 convert_element_type.3
  7.8 0.4 copy.24
  8.2 0.3 reshape.36.small
  8.5 1.4 %copy.27.bc_hbm = bf16[4096,32]{1,0:T(8,128)(2,1)S(1)} copy(bf16[4096,32]{0,1:T(8,128)(2,1)} %param.34) | data formatting | bytes 524288 | tf_op args[14]
  10.0 0.0 copy-done.4
  10.0 0.0 copy-done.3
  10.0 0.0 copy-done.7
  10.0 0.0 copy-done.1
  10.0 0.0 copy-done.26
  10.0 0.0 copy-done.25
  10.0 0.0 copy-start.27
  10.0 0.7 copy-done.27
  10.7 0.0 copy-start.28
  10.7 0.7 copy-done.28
  11.4 0.0 copy-start.29
  11.4 0.7 copy-done.29
  12.2 0.0 copy-start.30
  12.2 0.7 copy-done.30
  12.8 76.8 %exchange.1 = (f32[16,16,4096]{2,1,0:T(8,128)}, bf16[15,16,4096]{2,1,0:T(8,128)(2,1)}, bf16[2,16,16,128]{3,2,1,0:T(8,128)(2,1)S(1)}, f32[3,16,4096]{2,1,0:T(8,12...) custom-call(s32[128,2]{1,0:T(8,128)S(1)} %copy.25.moves, ...), custom_call_target="tpu_custom_call" | custom-call | tf_op jit(solution)/shard_map/exchange/pallas_call | solution.py:512
  89.6 0.0 copy-start.5
  89.6 0.9 copy-done.5
  90.5 0.0 copy-start.8
  90.5 0.7 copy-done.8
  91.2 0.0 copy-start.10
  91.2 0.7 copy-done.10
  91.9 0.0 copy-start.12
  91.9 0.7 copy-done.12
  92.6 0.7 copy-done.14
  93.3 0.0 copy-start.16
  93.3 0.6 copy-done.16
  94.0 0.7 copy-done.18
  94.6 0.7 copy-done.20
  95.3 0.7 copy-done.22
  95.9 0.6 copy-done.24
  96.6 0.6 copy-done.31
  97.2 1.6 %reshape.40 = bf16[2,16,2048]{2,1,0:T(8,128)(2,1)} reshape(bf16[2,16,16,128]{3,2,1,0:T(8,128)(2,1)} %copy-done.24) | data formatting | bytes 262144 | tf_op jit(solution)/shard_map/reshape | solution.py:612
  98.8 2.2 %copy-done = f32[16,16,4096]{2,1,0:T(8,128)S(1)} copy-done((f32[16,16,4096]{2,1,0:T(8,128)S(1)}, f32[16,16,4096]{2,1,0:T(8,128)}, u32[]{:S(2)}) %copy-start) | copy-done | bytes 4194328
  101.0 1.5 %copy-done.2 = bf16[15,16,4096]{2,1,0:T(8,128)(2,1)S(1)} copy-done((bf16[15,16,4096]{2,1,0:T(8,128)(2,1)S(1)}, bf16[15,16,4096]{2,1,0:T(8,128)(2,1)}, u32[]{:S(2)}) %copy-start.2) | copy-done | bytes 1966104
  102.5 0.9 copy-done.9
  103.5 0.9 copy-done.11
  104.4 0.9 copy-done.13
  105.4 0.9 copy-done.15
  106.3 0.9 copy-done.17
  107.2 0.9 copy-done.19
  108.1 0.9 copy-done.21
  109.0 0.9 copy-done.23
  109.9 0.7 copy-done.32
  110.6 8.0 %finish.1 = (f32[16,16,4096]{2,1,0:T(8,128)}, bf16[2,16,4096]{2,1,0:T(8,128)(2,1)}) custom-call(s32[32]{0:T(128)S(1)} %copy-done.32, f32[16,16,4096]{2,1,0:T(8,128)S(1)} %copy-done, bf16[15,16,4096]{2,1,0:T(8,128)(2,1)S(1)} %copy-done.2, f32[16,4096]{1,0:T(8,128)S(1)} %copy-done.9, f32[16,4096]{1,0:T(8,128)S(1)} %copy-done.11, ...), custom_call_target="tpu_custom_call" | custom-call | tf_op jit(solution)/shard_map/finish/pallas_call | solution.py:591
  118.6 0.0 copy-done.6
  118.6 0.9 copy.30
  (20 shorter events, 0.1 us)
Async XLA Ops:
  0.6 9.3 %copy-start.4 = (f32[16,4096]{1,0:T(8,128)S(1)}, f32[16,4096]{1,0:T(8,128)}, u32[]{:S(2)}) copy-start(f32[16,4096]{1,0:T(8,128)} %a_log.3) | copy-start | bytes 786436
  0.6 9.3 %copy-start.3 = (bf16[2,16,4096]{2,1,0:T(8,128)(2,1)S(1)}, bf16[2,16,4096]{2,1,0:T(8,128)(2,1)}, u32[]{:S(2)}) copy-start(bf16[2,16,4096]{2,1,0:T(8,128)(2,1)} %mz.3) | copy-start | bytes 786436
  0.7 9.3 %copy-start.7 = (bf16[2,16,4096]{2,1,0:T(8,128)(2,1)S(1)}, bf16[2,16,4096]{2,1,0:T(8,128)(2,1)}, u32[]{:S(2)}) copy-start(bf16[2,16,4096]{2,1,0:T(8,128)(2,1)} %mx.1) | copy-start | bytes 786436
  0.7 9.3 %copy-start.1 = (f32[16,3,4096]{2,0,1:T(8,128)S(1)}, f32[16,3,4096]{2,0,1:T(8,128)}, u32[]{:S(2)}) copy-start(f32[16,3,4096]{2,0,1:T(8,128)} %param.27) | copy-start | bytes 2359300
  0.7 9.3 %copy-start.26 = (f32[4096]{0:T(1024)S(1)}, f32[4096]{0:T(1024)}, u32[]{:S(2)}) copy-start(f32[4096]{0:T(1024)} %param.38) | copy-start | bytes 49156
  0.7 9.3 %copy-start.25 = (f32[4,4096]{1,0:T(4,128)S(1)}, f32[4,4096]{1,0:T(4,128)}, u32[]{:S(2)}) copy-start(f32[4,4096]{1,0:T(4,128)} %conv_w.1) | copy-start | bytes 196612
  10.0 0.7 copy-start.27
  10.7 0.7 copy-start.28
  11.4 0.7 copy-start.29
  12.2 0.7 copy-start.30
  89.6 0.9 copy-start.5
  90.5 0.7 copy-start.8
  91.2 0.7 copy-start.10
  91.9 0.7 copy-start.12
  92.6 0.7 copy-start.14
  93.3 0.7 copy-start.16
  94.0 0.7 copy-start.18
  94.6 0.7 copy-start.20
  95.3 0.7 copy-start.22
  95.9 0.6 copy-start.24
  96.6 0.6 copy-start.31
  98.8 2.2 %copy-start = (f32[16,16,4096]{2,1,0:T(8,128)S(1)}, f32[16,16,4096]{2,1,0:T(8,128)}, u32[]{:S(2)}) copy-start(f32[16,16,4096]{2,1,0:T(8,128)} %get-tuple-element.21.kept) | copy-start | bytes 12582916
  101.0 1.5 %copy-start.2 = (bf16[15,16,4096]{2,1,0:T(8,128)(2,1)S(1)}, bf16[15,16,4096]{2,1,0:T(8,128)(2,1)}, u32[]{:S(2)}) copy-start(bf16[15,16,4096]{2,1,0:T(8,128)(2,1)} %get-tuple-element.22.arrived) | copy-start | bytes 5898244
  102.5 0.9 copy-start.9
  103.5 0.9 copy-start.11
  104.4 0.9 copy-start.13
  105.4 0.9 copy-start.15
  106.3 0.9 copy-start.17
  107.2 0.9 copy-start.19
  108.1 0.9 copy-start.21
  109.0 0.9 copy-start.23
  109.9 0.7 copy-start.32
  110.6 8.0 %copy-start.6 = (f32[3,16,4096]{2,1,0:T(8,128)S(1)}, f32[3,16,4096]{2,1,0:T(8,128)}, u32[]{:S(2)}) copy-start(f32[3,16,4096]{2,1,0:T(8,128)} %copy-done.5) | copy-start | bytes 2359300

commit v3 on v2

v3 whole, which is shorter than its diff:
```python
import functools
import math

import jax
import jax.numpy as jnp
from jax import lax
from jax.experimental import pallas as pl
from jax.experimental.pallas import tpu as pltpu
from jax.sharding import PartitionSpec as P

HD = 128
F32, BF16 = jnp.float32, jnp.bfloat16
MESH = pl.DeviceIdType.MESH
ANY = pl.BlockSpec(memory_space=pl.ANY)
SMEM = pl.BlockSpec(memory_space=pltpu.SMEM)


def round_up(n, m):
    return (n + m - 1) // m * m


def silu(v):
    return v / (1.0 + jnp.exp(-v))


def softplus(v):
    return jnp.maximum(v, 0.0) + jnp.log1p(jnp.exp(-jnp.abs(v)))


def chunks(total, most=512):
    step = min(most, total)
    return [slice(i, i + step) for i in range(0, total, step)]


def exchange_kernel(
    sizes,
    moves,
    lengths,
    pages,
    conv_hbm,
    mx_hbm,
    q_hbm,
    nk_hbm,
    nv_hbm,
    states_hbm,
    keys_hbm,
    vals_hbm,
    conv_w_hbm,
    conv_b_hbm,
    down_hbm,
    bc_hbm,
    up_hbm,
    dt_b_hbm,
    a_log_hbm,
    skip_hbm,
    mz_hbm,
    state_one,
    got_state,
    att_out,
    fconv,
    m_one,
    vec_moved,
    b_moved,
    vec_two,
    bc_two,
    win,
    mx,
    queries,
    nk,
    nv,
    h,
    keys,
    vals,
    conv_w,
    conv_b,
    down,
    bc_w,
    up,
    dt_b,
    a_log,
    skip,
    mz,
    flat,
    asks,
    pack,
    send_state,
    send_small,
    got_small,
    send_ask,
    got_ask,
    att,
    att_two,
    send_att,
    got_att,
    win_two,
    xc_all,
    dt_all,
    b_all,
    c_all,
    xc_two,
    dt_two,
    b_two,
    c_two,
    rate,
    y,
    m_buf,
    part,
    part_two,
    load_sem,
    save_sem,
    state_s,
    state_r,
    small_s,
    small_r,
    ask_s,
    ask_r,
    att_s,
    att_r,
    part_s,
    part_r,
):
    R, T, S, L, H, KV = sizes
    C = h.shape[2]
    N = a_log.shape[0]
    NR = win.shape[1]
    rank = down.shape[1]
    page = keys.shape[1]
    n_pages = pages.shape[0]
    QW, W = queries.shape[2], keys.shape[2]
    A = asks.shape[2]
    me = lax.axis_index("replica")
    core = lax.axis_index("tensor")

    pairs = [(conv_hbm.at[k], win.at[k, pl.ds(0, S)]) for k in range(3)] + [
        (mx_hbm, mx),
        (q_hbm, queries),
        (nk_hbm, nk),
        (nv_hbm, nv),
        (states_hbm, h),
        (keys_hbm, keys),
        (vals_hbm, vals),
        (conv_w_hbm, conv_w),
        (conv_b_hbm, conv_b),
        (down_hbm, down),
        (bc_hbm, bc_w),
        (up_hbm, up),
        (dt_b_hbm, dt_b),
        (a_log_hbm, a_log),
        (skip_hbm, skip),
        (mz_hbm, mz),
    ]
    loads = [
        pltpu.make_async_copy(src, dst, load_sem.at[i]) for i, (src, dst) in enumerate(pairs)
    ]
    for load in loads:
        load.start()
    saves = []

    def save(src, dst):
        copy = pltpu.make_async_copy(src, dst, save_sem.at[len(saves)])
        copy.start()
        saves.append(copy)

    barrier = pltpu.get_barrier_semaphore()

    def greet(k, _):
        pl.semaphore_signal(
            barrier, inc=1, device_id={"replica": lax.rem(me + k, R)}, device_id_type=MESH
        )
        return 0

    def greet_core(k, _):
        pl.semaphore_signal(
            barrier, inc=1, device_id={"tensor": lax.rem(core + k, T)}, device_id_type=MESH
        )
        return 0

    lax.fori_loop(1, R, greet, 0)
    lax.fori_loop(1, T, greet_core, 0)

    shift = [lax.div(moves[1, j], S) for j in range(L)]
    out_slot = [lax.rem(moves[0, me * L + j], S) for j in range(L)]
    lane_of = [jnp.maximum(shift[j] - 1, 0) for j in range(L)]
    in_slot = [
        lax.rem(moves[1, lax.rem(me - shift[j] + R, R) * L + j], S) for j in range(L)
    ]

    def pick(values, k):
        found = values[0]
        for j in range(1, L):
            found = jnp.where(shift[j] == k, values[j], found)
        return found

    def source(g):
        row, lane = g, 0
        for j in range(L):
            hit = in_slot[j] == g
            row = jnp.where(hit, S + j, row)
            lane = jnp.where(hit, lane_of[j], lane)
        return row, lane

    def lane_copy(src, dst, send, recv, k, forward=True):
        to = lax.rem(me + k, R) if forward else lax.rem(me - k + R, R)
        return pltpu.make_async_remote_copy(
            src_ref=src.at[k - 1],
            dst_ref=dst.at[k - 1],
            send_sem=send.at[k - 1],
            recv_sem=recv.at[k - 1],
            device_id={"replica": to},
            device_id_type=MESH,
        )

    ask_copy = lambda k: lane_copy(send_ask, got_ask, ask_s, ask_r, k, False)
    small_copy = lambda k: lane_copy(send_small, got_small, small_s, small_r, k)
    state_copy = lambda k: lane_copy(send_state, got_state, state_s, state_r, k)
    att_copy = lambda k: lane_copy(send_att, got_att, att_s, att_r, k)

    for load in loads[4:7]:
        load.wait()
    for t in range(2):
        flat[t, :, :QW] = queries[t].astype(F32)
        flat[t, :, QW : QW + W] = nk[t].astype(F32)
        flat[t, :, QW + W :] = nv[t].astype(F32)

    def tile_up(g, _):
        for t in range(2):
            line = flat[t, pl.ds(g, 1), :]
            parts = [line[:, i * HD : (i + 1) * HD] for i in range(H + 2 * KV)]
            if A > H + 2 * KV:
                parts.append(jnp.zeros((A - H - 2 * KV, HD), F32))
            asks[t, g] = jnp.concatenate(parts, axis=0).astype(BF16)
        return 0

    lax.fori_loop(0, S, tile_up, 0)

    for load in loads[:4]:
        load.wait()
    win[3, :S] = mx[0].astype(F32)
    for j in range(L):
        lines = [win[k, pl.ds(out_slot[j], 1), :] for k in range(4)]
        pack[j] = jnp.concatenate(
            [line[:, i * (C // 4) : (i + 1) * (C // 4)] for line in lines for i in range(4)],
            axis=0,
        ).astype(BF16)

    pl.semaphore_wait(barrier, R - 1 + T - 1)

    def send_first(k, _):
        send_ask[k - 1] = asks[1, pick(in_slot, k)]
        ask_copy(k).start()
        send_small[k - 1] = pack[pick(range(L), k)]
        small_copy(k).start()
        return 0

    lax.fori_loop(1, R, send_first, 0)
    loads[7].wait()

    def send_states(k, _):
        slot = pick(out_slot, k)
        for c in chunks(C):
            send_state[k - 1, :, c] = h[slot, :, c].astype(BF16)
        state_copy(k).start()
        return 0

    lax.fori_loop(1, R, send_states, 0)

    loads[8].wait()
    loads[9].wait()
    lax.fori_loop(1, R, lambda k, _: (ask_copy(k).wait(), 0)[1], 0)

    rows = 2 * H
    head_of = lax.broadcasted_iota(jnp.int32, (rows, 1), 0) % H // (H // KV)
    step_of = lax.broadcasted_iota(jnp.int32, (rows, 1), 0) // H
    ask_col = lax.broadcasted_iota(jnp.int32, (rows, asks.shape[2]), 1)
    pos = lax.broadcasted_iota(jnp.int32, (rows, n_pages * page), 1)
    is_key = ask_col == H + head_of
    is_val = ask_col == H + KV + head_of
    nt = (((1,), (1,)), ((), ()))
    nn = (((1,), (0,)), ((), ()))

    def attend(g):
        length = lengths[me * S + g]
        gone = jnp.int32(0)
        lane = jnp.int32(0)
        for j in range(L):
            hit = out_slot[j] == g
            gone = jnp.where(hit, 1, gone)
            lane = jnp.where(hit, lane_of[j], lane)
        one = asks[0, g]
        two = jnp.where(gone == 1, got_ask[lane].astype(F32), asks[1, g].astype(F32)).astype(BF16)
        q = jnp.concatenate([one.astype(F32)[:H], two.astype(F32)[:H]], axis=0)
        qb = q.astype(BF16)
        wide = jnp.concatenate(
            [jnp.where(head_of == i, q, 0.0) for i in range(KV)], axis=1
        ).astype(BF16)
        scores = jnp.concatenate(
            [
                lax.dot_general(wide, keys[pages[p, g]], nt, preferred_element_type=F32)
                for p in range(n_pages)
            ],
            axis=1,
        )
        new_one = lax.dot_general(qb, one, nt, preferred_element_type=F32)
        new_two = lax.dot_general(qb, two, nt, preferred_element_type=F32)
        new_one = jnp.sum(jnp.where(is_key, new_one, 0.0), axis=1, keepdims=True)
        new_two = jnp.sum(jnp.where(is_key, new_two, 0.0), axis=1, keepdims=True)
        at_one, at_two = pos == length, pos == length + 1
        scores = jnp.where(at_one, new_one, jnp.where(at_two, new_two, scores))
        scores = scores * (1.0 / math.sqrt(HD))
        scores = jnp.where(pos <= length + step_of, scores, -1e30)
        expo = jnp.exp(scores - jnp.max(scores, axis=1, keepdims=True))
        w = expo / jnp.sum(expo, axis=1, keepdims=True)
        w_one = jnp.sum(jnp.where(at_one, w, 0.0), axis=1, keepdims=True)
        w_two = jnp.sum(jnp.where(at_two, w, 0.0), axis=1, keepdims=True)
        w = jnp.where(at_one | at_two, 0.0, w).astype(BF16)
        mixed = lax.dot_general(
            w[:, :page], vals[pages[0, g]], nn, preferred_element_type=F32
        )
        for p in range(1, n_pages):
            mixed += lax.dot_general(
                w[:, p * page : (p + 1) * page],
                vals[pages[p, g]],
                nn,
                preferred_element_type=F32,
            )
        out = lax.dot_general(
            jnp.where(is_val, w_one, 0.0).astype(BF16), one, nn, preferred_element_type=F32
        ) + lax.dot_general(
            jnp.where(is_val, w_two, 0.0).astype(BF16), two, nn, preferred_element_type=F32
        )
        for i in range(KV):
            out += jnp.where(head_of == i, mixed[:, i * HD : (i + 1) * HD], 0.0)
        first, second = out[:H], out[H:]
        if att.shape[2] > H:
            pad = jnp.zeros((att.shape[2] - H, HD), F32)
            first = jnp.concatenate([first, pad], axis=0)
            second = jnp.concatenate([second, pad], axis=0)
        return first.astype(BF16), second.astype(BF16)

    batch = 4 if S % 4 == 0 else 1

    def attend_some(i, _):
        results = [attend(i * batch + b) for b in range(batch)]
        for b, (first, second) in enumerate(results):
            att[0, i * batch + b] = first
            att_two[i * batch + b] = second
        return 0

    lax.fori_loop(0, S // batch, attend_some, 0)

    def send_back(k, _):
        send_att[k - 1] = att_two[pick(out_slot, k)]
        att_copy(k).start()
        return 0

    lax.fori_loop(1, R, send_back, 0)

    lax.fori_loop(1, R, lambda k, _: (small_copy(k).wait(), 0)[1], 0)
    for j in range(L):
        tile = got_small[lane_of[j]].astype(F32)
        for k in range(4):
            win[k, S + j : S + j + 1] = jnp.concatenate(
                [tile[4 * k + i : 4 * k + i + 1] for i in range(4)], axis=1
            )
    for k in range(4):
        win[k, S + L :] = jnp.zeros((NR - S - L, C), F32)

    def project(src, n, xc_ref, buf):
        low = jnp.zeros((n, rank), F32)
        bc = jnp.zeros((n, bc_w.shape[0]), F32)
        for c in chunks(C):
            total = conv_b[:, c] + src(0, c) * conv_w[0:1, c]
            for k in range(1, 4):
                total += src(k, c) * conv_w[k : k + 1, c]
            xb = silu(total).astype(BF16)
            xc_ref[:, c] = xb.astype(F32)
            low += lax.dot_general(xb, down[c], nn, preferred_element_type=F32)
            bc += lax.dot_general(xb, bc_w[:, c], nt, preferred_element_type=F32)
        buf[core, :, :rank] = low
        buf[core, :, rank:] = jnp.concatenate(
            [bc, jnp.zeros((n, HD - bc.shape[1]), F32)], axis=1
        )

    def core_copy(buf, which, k):
        return pltpu.make_async_remote_copy(
            src_ref=buf.at[core],
            dst_ref=buf.at[core],
            send_sem=part_s.at[which, k],
            recv_sem=part_r.at[which, k],
            device_id={"tensor": lax.rem(core + k, T)},
            device_id_type=MESH,
        )

    def reduce_parts(buf, which):
        lax.fori_loop(1, T, lambda k, _: (core_copy(buf, which, k).start(), 0)[1], 0)
        lax.fori_loop(1, T, lambda k, _: (core_copy(buf, which, k).wait(), 0)[1], 0)
        total = buf[0]
        for t in range(1, T):
            total += buf[t]
        return total

    def steps(total, n, dt_ref, b_ref, c_ref):
        low = total[:, :rank].astype(BF16)
        for c in chunks(C):
            dt_ref[:, c] = softplus(
                lax.dot_general(low, up[:, c], nn, preferred_element_type=F32) + dt_b[:, c]
            )
        turned = total[:, rank : rank + HD].T
        for i in range(n):
            b_ref[i] = jnp.broadcast_to(turned[:N, i : i + 1], (N, HD))
            c_ref[i] = jnp.broadcast_to(turned[N : 2 * N, i : i + 1], (N, HD))

    for load in loads[10:]:
        load.wait()
    rate[...] = jnp.exp(a_log[...])
    project(lambda k, c: win[k, :, c], NR, xc_all, part)
    steps(reduce_parts(part, 0), NR, dt_all, b_all, c_all)
    moved = pl.ds(S, NR - S)
    save(dt_all.at[moved], vec_moved.at[0])
    save(xc_all.at[moved], vec_moved.at[1])
    save(b_all.at[moved], b_moved)

    for g in range(S):
        row, _ = source(g)
        for k in range(3):
            win_two[k, g : g + 1] = win[k + 1, pl.ds(row, 1), :]
    win_two[3] = mx[1].astype(F32)
    save(win_two.at[pl.ds(1, 3)], fconv)
    project(lambda k, c: win_two[k, :, c], S, xc_two, part_two)
    steps(reduce_parts(part_two, 1), S, dt_two, b_two, c_two)
    save(dt_two, vec_two.at[0])
    save(xc_two, vec_two.at[1])
    save(b_two, bc_two.at[0])
    save(c_two, bc_two.at[1])

    def scan(g, _):
        for c in chunks(C, 2048):
            reps = (c.stop - c.start) // HD
            dt = dt_all[pl.ds(g, 1), c]
            x = xc_all[pl.ds(g, 1), c]
            new = jnp.exp(-dt * rate[:, c]) * h[g, :, c]
            new += jnp.concatenate([b_all[g]] * reps, axis=1) * (dt * x)
            line = jnp.sum(jnp.concatenate([c_all[g]] * reps, axis=1) * new, axis=0, keepdims=True)
            h[g, :, c] = new
            y[pl.ds(g, 1), c] = line
        return 0

    lax.fori_loop(0, S, scan, 0)
    save(h, state_one)
    for c in chunks(C):
        m_buf[:, c] = (
            (y[:, c] + skip[:, c] * xc_all[:S, c]) * silu(mz[0, :, c].astype(F32))
        ).astype(BF16)

    save(m_buf, m_one)

    lax.fori_loop(1, R, lambda k, _: (att_copy(k).wait(), 0)[1], 0)
    for g in range(S):
        row, lane = source(g)
        att[1, g] = jnp.where(
            row >= S, got_att[lane].astype(F32), att_two[g].astype(F32)
        ).astype(BF16)
    save(att, att_out)
    for copy in saves:
        copy.wait()
    lax.fori_loop(1, R, lambda k, _: (state_copy(k).wait(), 0)[1], 0)


def arrival(moves, me, g, R, S, L):
    row, lane = g, 0
    for j in range(L):
        shift = lax.div(moves[1, j], S)
        slot = lax.rem(moves[1, lax.rem(me - shift + R, R) * L + j], S)
        row = jnp.where(slot == g, S + j, row)
        lane = jnp.where(slot == g, jnp.maximum(shift - 1, 0), lane)
    return row, lane


def finish_kernel(
    sizes,
    moves,
    here,
    kept,
    arrived,
    vec_moved,
    b_moved,
    vec_two,
    bc_two,
    a_log,
    skip,
    mz,
    m_one,
    final,
    out,
    rate,
    y,
):
    R, S, L = sizes
    C = final.shape[2]
    g = pl.program_id(0)
    row, _ = arrival(moves, here[0], g, R, S, L)
    wide = lambda v, c: jnp.concatenate([v] * ((c.stop - c.start) // HD), axis=1)

    @pl.when(g == 0)
    def _():
        rate[...] = jnp.exp(a_log[...])
        out[0] = m_one[...]

    def second(prev, c):
        dt, x = vec_two[0, pl.ds(g, 1), c], vec_two[1, pl.ds(g, 1), c]
        new = jnp.exp(-dt * rate[:, c]) * prev + wide(bc_two[0, g], c) * (dt * x)
        line = jnp.sum(wide(bc_two[1, g], c) * new, axis=0, keepdims=True)
        final[0, :, c] = new
        y[pl.ds(g, 1), c] = line

    @pl.when(row < S)
    def _():
        for c in chunks(C, 2048):
            second(kept[0, :, c], c)

    @pl.when(row >= S)
    def _():
        j = row - S
        for c in chunks(C, 2048):
            dt, x = vec_moved[0, pl.ds(j, 1), c], vec_moved[1, pl.ds(j, 1), c]
            one = jnp.exp(-dt * rate[:, c]) * arrived[0, :, c].astype(F32)
            second(one + wide(b_moved[j], c) * (dt * x), c)

    @pl.when(g == S - 1)
    def _():
        for c in chunks(C):
            out[1, :, c] = (
                (y[:, c] + skip[:, c] * vec_two[1, :, c]) * silu(mz[1, :, c].astype(F32))
            ).astype(BF16)


def shards(
    lengths,
    page_table,
    key_pool,
    value_pool,
    queries,
    new_keys,
    new_values,
    conv_state,
    ssm_state,
    mamba_x,
    mamba_z,
    conv_weight,
    conv_bias,
    dt_down,
    bc_proj,
    dt_up,
    dt_bias,
    a_log,
    skip_d,
    moves,
):
    R, T = lax.axis_size("replica"), lax.axis_size("tensor")
    S, N, C = ssm_state.shape
    L = moves.shape[0] // R
    QW, W = queries.shape[2], key_pool.shape[2]
    H, KV = QW // HD, W // HD
    A = round_up(H + 2 * KV, 16)
    AH = round_up(H, 16)
    NR = S + round_up(L, 16)
    rank = dt_down.shape[1]

    row = lambda v: v.reshape(1, C)
    shape = jax.ShapeDtypeStruct
    dma = pltpu.SemaphoreType.DMA
    vm = lambda dims, kind=F32: pltpu.VMEM(dims, kind)
    like = lambda v: pltpu.VMEM(v.shape, v.dtype)
    NM = NR - S
    turned = moves.T
    operands = (
        jnp.transpose(conv_state, (1, 0, 2)),
        mamba_x,
        queries,
        new_keys,
        new_values,
        ssm_state,
        key_pool,
        value_pool,
        conv_weight,
        row(conv_bias),
        dt_down,
        bc_proj.T,
        dt_up,
        row(dt_bias),
        a_log,
        row(skip_d),
        mamba_z,
    )
    state_one, got_state, att, fconv, m_one, *rest = pl.pallas_call(
        functools.partial(exchange_kernel, (R, T, S, L, H, KV)),
        out_shape=(
            shape((S, N, C), F32),
            shape((R - 1, N, C), BF16),
            shape((2, S, AH, HD), BF16),
            shape((3, S, C), F32),
            shape((S, C), BF16),
            shape((2, NM, C), F32),
            shape((NM, N, HD), F32),
            shape((2, S, C), F32),
            shape((2, S, N, HD), F32),
        ),
        in_specs=[SMEM] * 3 + [ANY] * len(operands),
        out_specs=(ANY,) * 9,
        scratch_shapes=[vm((4, NR, C))]
        + [like(v) for v in operands[1:]]
        + [
            vm((2, S, QW + 2 * W)),
            vm((2, S, A, HD), BF16),
            vm((L, 16, C // 4), BF16),
            vm((R - 1, N, C), BF16),
            vm((R - 1, 16, C // 4), BF16),
            vm((R - 1, 16, C // 4), BF16),
            vm((R - 1, A, HD), BF16),
            vm((R - 1, A, HD), BF16),
            vm((2, S, AH, HD), BF16),
            vm((S, AH, HD), BF16),
            vm((R - 1, AH, HD), BF16),
            vm((R - 1, AH, HD), BF16),
            vm((4, S, C)),
            vm((NR, C)),
            vm((NR, C)),
            vm((NR, N, HD)),
            vm((NR, N, HD)),
            vm((S, C)),
            vm((S, C)),
            vm((S, N, HD)),
            vm((S, N, HD)),
            vm((N, C)),
            vm((S, C)),
            vm((S, C), BF16),
            vm((T, NR, rank + HD)),
            vm((T, S, rank + HD)),
            dma((len(operands) + 2,)),
            dma((11,)),
        ]
        + [dma((R - 1,))] * 8
        + [dma((2, T))] * 2,
        compiler_params=pltpu.CompilerParams(
            collective_id=0, has_side_effects=True, vmem_limit_bytes=58 * 1024 * 1024
        ),
        name="exchange",
    )(turned, lengths, page_table.T, *operands)
    whole = lambda v: pl.BlockSpec(v.shape, lambda g, m, i: (0,) * v.ndim)
    rest = rest + [a_log, row(skip_d), mamba_z, m_one]
    here = jnp.full((1,), lax.axis_index("replica"), jnp.int32)
    final_ssm, mamba_out = pl.pallas_call(
        functools.partial(finish_kernel, (R, S, L)),
        grid_spec=pltpu.PrefetchScalarGridSpec(
            num_scalar_prefetch=2,
            grid=(S,),
            in_specs=[
                pl.BlockSpec((1, N, C), lambda g, m, i: (g, 0, 0)),
                pl.BlockSpec((1, N, C), lambda g, m, i: (arrival(m, i[0], g, R, S, L)[1], 0, 0)),
            ]
            + [whole(v) for v in rest],
            out_specs=[
                pl.BlockSpec((1, N, C), lambda g, m, i: (g, 0, 0)),
                pl.BlockSpec((2, S, C), lambda g, m, i: (0, 0, 0)),
            ],
            scratch_shapes=[pltpu.VMEM((N, C), F32), pltpu.VMEM((S, C), F32)],
        ),
        out_shape=(shape((S, N, C), F32), shape((2, S, C), BF16)),
        compiler_params=pltpu.CompilerParams(vmem_limit_bytes=58 * 1024 * 1024),
        name="finish",
    )(turned, here, state_one, got_state, *rest)
    return (
        att[:, :, :H].reshape(2, S, QW),
        mamba_out,
        final_ssm,
        jnp.transpose(fconv, (1, 0, 2)),
    )


def solution(mesh):
    row, both = P("replica", None, "tensor"), P(None, "replica", "tensor")
    in_specs = (
        P(),
        P("replica", None),
        row,
        row,
        both,
        both,
        both,
        row,
        row,
        both,
        both,
        P(None, "tensor"),
        P("tensor"),
        P("tensor", None),
        P("tensor", None),
        P(None, "tensor"),
        P("tensor"),
        P(None, "tensor"),
        P("tensor"),
        P(),
    )
    return jax.shard_map(
        shards, mesh=mesh, in_specs=in_specs, out_specs=(both, both, row, row), check_vma=False
    )
```

time: 120 us -> 90.6 us (0.76)
  local copies, waits for them, and re-layouts: 32.5 us -> 2.5 us
  Pallas kernels: 84.8 us -> 87 us
  other arithmetic: 1.34 us -> 0 us
    unnamed x71 -> x3, local copies, waits for them, and re-layouts: 27.6 us -> 0.89 us
    pallas_call x1, Pallas kernels: 7.99 us -> 13.8 us  [shards(): pl.pallas_call(functools.partial(finish_kernel, (R, S, L)), grid_spec=plt...]
    pallas_call x1, Pallas kernels: 76.8 us -> 73.2 us  [shards(): pl.pallas_call(functools.partial(exchange_kernel, (R, T, S, L, H, KV)), o...]
    reshape x3 -> x0, local copies, waits for them, and re-layouts: 1.88 us -> none  [the longest x2 1.54 us: shards(): heads = lambda t: t.reshape(2, S, -1, HD)]
where the time goes in v3:
time: 90.6 us; the launch traced here: 90.1 us
  Pallas kernels  87 us (96%)
  local copies, waits for them, and re-layouts  2.5 us (3%)
    pallas_call x1, Pallas kernels, shards(): pl.pallas_call(functools.partial(exchange_kernel, (R, T, S, L, H, KV)), o...  73.2 us
    pallas_call x1, Pallas kernels, shards(): pl.pallas_call(functools.partial(finish_kernel, (R, S, L)), grid_spec=plt...  13.8 us

profile of v3, /device:TPU:0, one launch (start us, length us, event | category | flops | bytes accessed | tf_op | source)
XLA Modules:
  0.0 90.1 jit_solution(3226881506775147292)
XLA Ops:
  0.6 73.2 %exchange.1 = (f32[16,16,4096]{2,1,0:T(8,128)}, bf16[15,16,4096]{2,1,0:T(8,128)(2,1)}, bf16[2,16,16,128]{3,2,1,0:T(8,128)(2,1)}, f32[3,16,4096]{2,1,0:T(8,128)},...) custom-call(s32[2,128]{1,0:T(2,128)} %bitcast.18, ...), custom_call_target="tpu_custom_call" | custom-call | tf_op jit(solution)/shard_map/exchange/pallas_call | solution.py:595
  73.8 1.6 %reshape.24 = bf16[2,16,2048]{2,1,0:T(8,128)(2,1)} reshape(bf16[2,16,16,128]{3,2,1,0:T(8,128)(2,1)} %get-tuple-element.15) | data formatting | bytes 262144 | tf_op jit(solution)/shard_map/reshape | solution.py:673
  75.4 0.0 copy-start
  75.4 13.8 %finish.1 = (f32[16,16,4096]{2,1,0:T(8,128)}, bf16[2,16,4096]{2,1,0:T(8,128)(2,1)}) custom-call(s32[2,128]{1,0:T(2,128)} %bitcast.19, s32[1]{0:T(128)} %bitcast.7.here, f32[16,16,4096]{2,1,0:T(8,128)} %get-tuple-element.16.kept, bf16[15,16,4096]{2,1,0:T(8,128)(2,1)} %get-tuple-element.17.arrived, f32[2,16,4096]{2,1,0:T(8,128)} %get-tuple-element.18.vec_moved, ...), custom_call_target="tpu_custom_call" | custom-call | tf_op jit(solution)/shard_map/finish/pallas_call | solution.py:652
  89.2 0.0 copy-done
  89.2 0.9 copy.25
Async XLA Ops:
  75.4 13.8 %copy-start = (f32[3,16,4096]{2,1,0:T(8,128)S(1)}, f32[3,16,4096]{2,1,0:T(8,128)}, u32[]{:S(2)}) copy-start(f32[3,16,4096]{2,1,0:T(8,128)} %get-tuple-element.25) | copy-start | bytes 2359300

commit v4 on v3

--- a/solution.py
+++ b/solution.py
@@ -54,7 +54,7 @@
     a_log_hbm,
     skip_hbm,
     mz_hbm,
-    state_one,
+    stay_out,
     got_state,
     att_out,
     fconv,
@@ -63,6 +63,7 @@
     b_moved,
     vec_two,
     bc_two,
+    y_out,
     win,
     mx,
     queries,
@@ -88,7 +89,6 @@
     got_small,
     send_ask,
     got_ask,
-    att,
     att_two,
     send_att,
     got_att,
@@ -103,6 +103,10 @@
     c_two,
     rate,
     y,
+    y_stay,
+    stay,
+    att_flat,
+    att_bf,
     m_buf,
     part,
     part_two,
@@ -278,6 +282,9 @@
     nt = (((1,), (1,)), ((), ()))
     nn = (((1,), (0,)), ((), ()))
 
+    def line_up(tile):
+        return jnp.concatenate([tile[i : i + 1] for i in range(H)], axis=1)
+
     def attend(g):
         length = lengths[me * S + g]
         gone = jnp.int32(0)
@@ -331,8 +338,8 @@
         for i in range(KV):
             out += jnp.where(head_of == i, mixed[:, i * HD : (i + 1) * HD], 0.0)
         first, second = out[:H], out[H:]
-        if att.shape[2] > H:
-            pad = jnp.zeros((att.shape[2] - H, HD), F32)
+        if att_two.shape[1] > H:
+            pad = jnp.zeros((att_two.shape[1] - H, HD), F32)
             first = jnp.concatenate([first, pad], axis=0)
             second = jnp.concatenate([second, pad], axis=0)
         return first.astype(BF16), second.astype(BF16)
@@ -342,7 +349,7 @@
     def attend_some(i, _):
         results = [attend(i * batch + b) for b in range(batch)]
         for b, (first, second) in enumerate(results):
-            att[0, i * batch + b] = first
+            att_flat[0, pl.ds(i * batch + b, 1), :] = line_up(first.astype(F32))
             att_two[i * batch + b] = second
         return 0
 
@@ -446,7 +453,27 @@
         return 0
 
     lax.fori_loop(0, S, scan, 0)
-    save(h, state_one)
+
+    stay_slots = staying(out_slot, S, S - L)
+
+    def scan_stay(i, _):
+        g = stay_slots[0]
+        for n in range(1, S - L):
+            g = jnp.where(i == n, stay_slots[n], g)
+        for c in chunks(C, 2048):
+            reps = (c.stop - c.start) // HD
+            dt = dt_two[pl.ds(g, 1), c]
+            x = xc_two[pl.ds(g, 1), c]
+            new = jnp.exp(-dt * rate[:, c]) * h[g, :, c]
+            new += jnp.concatenate([b_two[g]] * reps, axis=1) * (dt * x)
+            line = jnp.sum(jnp.concatenate([c_two[g]] * reps, axis=1) * new, axis=0, keepdims=True)
+            stay[i, :, c] = new
+            y_stay[pl.ds(i, 1), c] = line
+        return 0
+
+    lax.fori_loop(0, S - L, scan_stay, 0)
+    save(stay, stay_out)
+    save(y_stay, y_out)
     for c in chunks(C):
         m_buf[:, c] = (
             (y[:, c] + skip[:, c] * xc_all[:S, c]) * silu(mz[0, :, c].astype(F32))
@@ -457,81 +484,137 @@
     lax.fori_loop(1, R, lambda k, _: (att_copy(k).wait(), 0)[1], 0)
     for g in range(S):
         row, lane = source(g)
-        att[1, g] = jnp.where(
-            row >= S, got_att[lane].astype(F32), att_two[g].astype(F32)
-        ).astype(BF16)
-    save(att, att_out)
+        tile = jnp.where(row >= S, got_att[lane].astype(F32), att_two[g].astype(F32))
+        att_flat[1, g : g + 1] = line_up(tile)
+    att_bf[...] = att_flat[...].astype(BF16)
+    save(att_bf, att_out)
     for copy in saves:
         copy.wait()
     lax.fori_loop(1, R, lambda k, _: (state_copy(k).wait(), 0)[1], 0)
 
 
-def arrival(moves, me, g, R, S, L):
-    row, lane = g, 0
-    for j in range(L):
-        shift = lax.div(moves[1, j], S)
-        slot = lax.rem(moves[1, lax.rem(me - shift + R, R) * L + j], S)
-        row = jnp.where(slot == g, S + j, row)
-        lane = jnp.where(slot == g, jnp.maximum(shift - 1, 0), lane)
-    return row, lane
-
-
 def finish_kernel(
     sizes,
     moves,
-    here,
-    kept,
+    stay,
+    got_state,
+    att_in,
+    fconv_in,
+    m_one,
+    vec_moved_hbm,
+    b_moved_hbm,
+    vec_two_hbm,
+    bc_two_hbm,
+    y_hbm,
+    a_log_hbm,
+    skip_hbm,
+    mz_hbm,
+    att,
+    out,
+    final,
+    fconv,
     arrived,
+    done,
     vec_moved,
     b_moved,
     vec_two,
     bc_two,
-    a_log,
+    y_stay,
+    rate,
     skip,
     mz,
-    m_one,
-    final,
-    out,
-    rate,
     y,
+    m_two,
+    load_sem,
+    arrive_sem,
+    stay_sem,
+    done_sem,
+    pass_sem,
 ):
     R, S, L = sizes
     C = final.shape[2]
-    g = pl.program_id(0)
-    row, _ = arrival(moves, here[0], g, R, S, L)
+    me = lax.axis_index("replica")
+    shift = [lax.div(moves[1, j], S) for j in range(L)]
+    slot = [lax.rem(moves[1, lax.rem(me - shift[j] + R, R) * L + j], S) for j in range(L)]
+    pairs = [
+        (a_log_hbm, rate),
+        (vec_moved_hbm, vec_moved),
+        (b_moved_hbm, b_moved),
+        (vec_two_hbm, vec_two),
+        (bc_two_hbm, bc_two),
+        (y_hbm, y_stay),
+        (skip_hbm, skip),
+        (mz_hbm, mz),
+    ]
+    loads = [
+        pltpu.make_async_copy(src, dst, load_sem.at[i]) for i, (src, dst) in enumerate(pairs)
+    ]
+    arrivals = [
+        pltpu.make_async_copy(
+            got_state.at[jnp.maximum(shift[j] - 1, 0)], arrived.at[j], arrive_sem.at[j]
+        )
+        for j in range(L)
+    ]
+    for load in loads[:5]:
+        load.start()
+    for copy in arrivals:
+        copy.start()
+    for load in loads[5:]:
+        load.start()
+    stay_slots = staying(slot, S, S - L)
+    passes = [
+        pltpu.make_async_copy(stay.at[i], final.at[stay_slots[i]], stay_sem.at[i])
+        for i in range(S - L)
+    ] + [
+        pltpu.make_async_copy(att_in, att, pass_sem.at[0]),
+        pltpu.make_async_copy(fconv_in, fconv, pass_sem.at[1]),
+        pltpu.make_async_copy(m_one, out.at[0], pass_sem.at[2]),
+    ]
+    for copy in passes:
+        copy.start()
     wide = lambda v, c: jnp.concatenate([v] * ((c.stop - c.start) // HD), axis=1)
-
-    @pl.when(g == 0)
-    def _():
-        rate[...] = jnp.exp(a_log[...])
-        out[0] = m_one[...]
-
-    def second(prev, c):
-        dt, x = vec_two[0, pl.ds(g, 1), c], vec_two[1, pl.ds(g, 1), c]
-        new = jnp.exp(-dt * rate[:, c]) * prev + wide(bc_two[0, g], c) * (dt * x)
-        line = jnp.sum(wide(bc_two[1, g], c) * new, axis=0, keepdims=True)
-        final[0, :, c] = new
-        y[pl.ds(g, 1), c] = line
-
-    @pl.when(row < S)
-    def _():
-        for c in chunks(C, 2048):
-            second(kept[0, :, c], c)
-
-    @pl.when(row >= S)
-    def _():
-        j = row - S
-        for c in chunks(C, 2048):
-            dt, x = vec_moved[0, pl.ds(j, 1), c], vec_moved[1, pl.ds(j, 1), c]
-            one = jnp.exp(-dt * rate[:, c]) * arrived[0, :, c].astype(F32)
-            second(one + wide(b_moved[j], c) * (dt * x), c)
-
-    @pl.when(g == S - 1)
-    def _():
-        for c in chunks(C):
-            out[1, :, c] = (
-                (y[:, c] + skip[:, c] * vec_two[1, :, c]) * silu(mz[1, :, c].astype(F32))
-            ).astype(BF16)
+    for load in loads:
+        load.wait()
+    rate[...] = jnp.exp(rate[...])
+    for i in range(S - L):
+        y[pl.ds(stay_slots[i], 1), :] = y_stay[i : i + 1]
+    results = []
+    for j in range(L):
+        g = slot[j]
+        arrivals[j].wait()
+        for c in chunks(C, 1024):
+            dt, x = vec_moved[0, j : j + 1, c], vec_moved[1, j : j + 1, c]
+            new = jnp.exp(-dt * rate[:, c]) * arrived[j, :, c].astype(F32)
+            new += wide(b_moved[j], c) * (dt * x)
+            dt, x = vec_two[0, pl.ds(g, 1), c], vec_two[1, pl.ds(g, 1), c]
+            new = jnp.exp(-dt * rate[:, c]) * new + wide(bc_two[0, g], c) * (dt * x)
+            line = jnp.sum(wide(bc_two[1, g], c) * new, axis=0, keepdims=True)
+            done[j, :, c] = new
+            y[pl.ds(g, 1), c] = line
+        copy = pltpu.make_async_copy(done.at[j], final.at[g], done_sem.at[j])
+        copy.start()
+        results.append(copy)
+    for c in chunks(C):
+        m_two[:, c] = (
+            (y[:, c] + skip[:, c] * vec_two[1, :, c]) * silu(mz[1, :, c].astype(F32))
+        ).astype(BF16)
+    last = pltpu.make_async_copy(m_two, out.at[1], pass_sem.at[3])
+    last.start()
+    for copy in passes + results + [last]:
+        copy.wait()
+
+
+def staying(moved, slots, count):
+    found = [jnp.int32(0)] * count
+    seen = jnp.int32(0)
+    for g in range(slots):
+        gone = moved[0] == g
+        for slot in moved[1:]:
+            gone = gone | (slot == g)
+        for i in range(count):
+            found[i] = jnp.where(~gone & (seen == i), g, found[i])
+        seen = seen + jnp.where(gone, 0, 1)
+    return found
 
 
 def shards(
@@ -592,21 +675,22 @@
         row(skip_d),
         mamba_z,
     )
-    state_one, got_state, att, fconv, m_one, *rest = pl.pallas_call(
+    results = pl.pallas_call(
         functools.partial(exchange_kernel, (R, T, S, L, H, KV)),
         out_shape=(
-            shape((S, N, C), F32),
+            shape((S - L, N, C), F32),
             shape((R - 1, N, C), BF16),
-            shape((2, S, AH, HD), BF16),
+            shape((2, S, QW), BF16),
             shape((3, S, C), F32),
             shape((S, C), BF16),
             shape((2, NM, C), F32),
             shape((NM, N, HD), F32),
             shape((2, S, C), F32),
             shape((2, S, N, HD), F32),
+            shape((S - L, C), F32),
         ),
         in_specs=[SMEM] * 3 + [ANY] * len(operands),
-        out_specs=(ANY,) * 9,
+        out_specs=(ANY,) * 10,
         scratch_shapes=[vm((4, NR, C))]
         + [like(v) for v in operands[1:]]
         + [
@@ -618,7 +702,6 @@
             vm((R - 1, 16, C // 4), BF16),
             vm((R - 1, A, HD), BF16),
             vm((R - 1, A, HD), BF16),
-            vm((2, S, AH, HD), BF16),
             vm((S, AH, HD), BF16),
             vm((R - 1, AH, HD), BF16),
             vm((R - 1, AH, HD), BF16),
@@ -633,11 +716,15 @@
             vm((S, N, HD)),
             vm((N, C)),
             vm((S, C)),
+            vm((S - L, C)),
+            vm((S - L, N, C)),
+            vm((2, S, QW)),
+            vm((2, S, QW), BF16),
             vm((S, C), BF16),
             vm((T, NR, rank + HD)),
             vm((T, S, rank + HD)),
             dma((len(operands) + 2,)),
-            dma((11,)),
+            dma((12,)),
         ]
         + [dma((R - 1,))] * 8
         + [dma((2, T))] * 2,
@@ -646,35 +733,39 @@
         ),
         name="exchange",
     )(turned, lengths, page_table.T, *operands)
-    whole = lambda v: pl.BlockSpec(v.shape, lambda g, m, i: (0,) * v.ndim)
-    rest = rest + [a_log, row(skip_d), mamba_z, m_one]
-    here = jnp.full((1,), lax.axis_index("replica"), jnp.int32)
-    final_ssm, mamba_out = pl.pallas_call(
+    att, mamba_out, final_ssm, fconv = pl.pallas_call(
         functools.partial(finish_kernel, (R, S, L)),
-        grid_spec=pltpu.PrefetchScalarGridSpec(
-            num_scalar_prefetch=2,
-            grid=(S,),
-            in_specs=[
-                pl.BlockSpec((1, N, C), lambda g, m, i: (g, 0, 0)),
-                pl.BlockSpec((1, N, C), lambda g, m, i: (arrival(m, i[0], g, R, S, L)[1], 0, 0)),
-            ]
-            + [whole(v) for v in rest],
-            out_specs=[
-                pl.BlockSpec((1, N, C), lambda g, m, i: (g, 0, 0)),
-                pl.BlockSpec((2, S, C), lambda g, m, i: (0, 0, 0)),
-            ],
-            scratch_shapes=[pltpu.VMEM((N, C), F32), pltpu.VMEM((S, C), F32)],
+        in_specs=[SMEM] + [ANY] * 13,
+        out_specs=[ANY] * 4,
+        out_shape=(
+            shape((2, S, QW), BF16),
+            shape((2, S, C), BF16),
+            shape((S, N, C), F32),
+            shape((3, S, C), F32),
         ),
-        out_shape=(shape((S, N, C), F32), shape((2, S, C), BF16)),
+        scratch_shapes=[
+            vm((L, N, C), BF16),
+            vm((L, N, C)),
+            vm((2, NM, C)),
+            vm((NM, N, HD)),
+            vm((2, S, C)),
+            vm((2, S, N, HD)),
+            vm((S - L, C)),
+            vm((N, C)),
+            vm((1, C)),
+            vm((2, S, C), BF16),
+            vm((S, C)),
+            vm((S, C), BF16),
+            dma((8,)),
+            dma((L,)),
+            dma((S - L,)),
+            dma((L,)),
+            dma((4,)),
+        ],
         compiler_params=pltpu.CompilerParams(vmem_limit_bytes=58 * 1024 * 1024),
         name="finish",
-    )(turned, here, state_one, got_state, *rest)
-    return (
-        att[:, :, :H].reshape(2, S, QW),
-        mamba_out,
-        final_ssm,
-        jnp.transpose(fconv, (1, 0, 2)),
-    )
+    )(turned, *results, a_log, row(skip_d), mamba_z)
+    return att, mamba_out, final_ssm, jnp.transpose(fconv, (1, 0, 2))
 
 
 def solution(mesh):

time: 90.6 us -> 172 us (1.90)
  Pallas kernels: 87 us -> 171 us
  local copies, waits for them, and re-layouts: 2.5 us -> 0 us
    pallas_call x1, Pallas kernels: 13.8 us -> 97.7 us  [shards(): pl.pallas_call(functools.partial(finish_kernel, (R, S, L)), in_specs=[SME...]
where the time goes in v4:
time: 172 us
  Pallas kernels  171 us (99%)
    pallas_call x1, Pallas kernels, shards(): pl.pallas_call(functools.partial(finish_kernel, (R, S, L)), in_specs=[SME...  97.7 us
    pallas_call x1, Pallas kernels, shards(): pl.pallas_call(functools.partial(exchange_kernel, (R, T, S, L, H, KV)), o...  73.2 us

profile of v4, /device:TPU:0, one launch (start us, length us, event | category | flops | bytes accessed | tf_op | source)
XLA Modules:
  0.0 171.6 jit_solution(6011139061419897543)
XLA Ops:
  0.6 73.2 %exchange.1 = (f32[8,16,4096]{2,1,0:T(8,128)}, bf16[15,16,4096]{2,1,0:T(8,128)(2,1)}, bf16[2,16,2048]{2,1,0:T(8,128)(2,1)}, f32[3,16,4096]{2,1,0:T(8,128)}, bf16...) custom-call(s32[2,128]{1,0:T(2,128)} %bitcast.14, ...), custom_call_target="tpu_custom_call" | custom-call | tf_op jit(solution)/shard_map/exchange/pallas_call | solution.py:678
  73.8 97.7 %finish.1 = (bf16[2,16,2048]{2,1,0:T(8,128)(2,1)}, bf16[2,16,4096]{2,1,0:T(8,128)(2,1)}, f32[16,16,4096]{2,1,0:T(8,128)}, f32[3,16,4096]{2,1,0:T(8,128)}) custom-call(s32[2,128]{1,0:T(2,128)} %bitcast.15, f32[8,16,4096]{2,1,0:T(8,128)} %get-tuple-element.18.stay, bf16[15,16,4096]{2,1,0:T(8,128)(2,1)} %get-tuple-element.19.got_state, ...), custom_call_target="tpu_custom_call" | custom-call | tf_op jit(solution)/shard_map/finish/pallas_call | solution.py:736

commit v5 on v4

--- a/solution.py
+++ b/solution.py
@@ -156,7 +156,8 @@
     loads = [
         pltpu.make_async_copy(src, dst, load_sem.at[i]) for i, (src, dst) in enumerate(pairs)
     ]
-    for load in loads:
+    loads[7].start()
+    for load in loads[:7] + loads[8:]:
         load.start()
     saves = []
 
@@ -219,6 +220,35 @@
     state_copy = lambda k: lane_copy(send_state, got_state, state_s, state_r, k)
     att_copy = lambda k: lane_copy(send_att, got_att, att_s, att_r, k)
 
+    pl.semaphore_wait(barrier, R - 1 + T - 1)
+
+    def lane(i):
+        return 1 + lax.rem(7 * i, R - 1)
+
+    def send_states(i, _):
+        k = lane(i)
+        slot = pick(out_slot, k)
+        for c in chunks(C):
+            send_state[k - 1, :, c] = h[slot, :, c].astype(BF16)
+        state_copy(k).start()
+        return 0
+
+    def send_small_rows(i, _):
+        k = lane(i)
+        send_small[k - 1] = pack[pick(range(L), k)]
+        small_copy(k).start()
+        return 0
+
+    def send_asks(i, _):
+        k = lane(i)
+        send_ask[k - 1] = asks[1, pick(in_slot, k)]
+        ask_copy(k).start()
+        return 0
+
+    early = min(4, R - 1)
+    loads[7].wait()
+    lax.fori_loop(0, early, send_states, 0)
+
     for load in loads[4:7]:
         load.wait()
     for t in range(2):
@@ -247,26 +277,9 @@
             axis=0,
         ).astype(BF16)
 
-    pl.semaphore_wait(barrier, R - 1 + T - 1)
-
-    def send_first(k, _):
-        send_ask[k - 1] = asks[1, pick(in_slot, k)]
-        ask_copy(k).start()
-        send_small[k - 1] = pack[pick(range(L), k)]
-        small_copy(k).start()
-        return 0
-
-    lax.fori_loop(1, R, send_first, 0)
-    loads[7].wait()
-
-    def send_states(k, _):
-        slot = pick(out_slot, k)
-        for c in chunks(C):
-            send_state[k - 1, :, c] = h[slot, :, c].astype(BF16)
-        state_copy(k).start()
-        return 0
-
-    lax.fori_loop(1, R, send_states, 0)
+    lax.fori_loop(0, R - 1, send_asks, 0)
+    lax.fori_loop(0, R - 1, send_small_rows, 0)
+    lax.fori_loop(early, R - 1, send_states, 0)
 
     loads[8].wait()
     loads[9].wait()
@@ -525,6 +538,11 @@
     mz,
     y,
     m_two,
+    stay_v,
+    att_v,
+    fconv_v,
+    m_v,
+    first_sem,
     load_sem,
     arrive_sem,
     stay_sem,
@@ -561,21 +579,31 @@
         copy.start()
     for load in loads[5:]:
         load.start()
+    firsts = [
+        pltpu.make_async_copy(src, dst, first_sem.at[i])
+        for i, (src, dst) in enumerate(
+            [(stay, stay_v), (att_in, att_v), (fconv_in, fconv_v), (m_one, m_v)]
+        )
+    ]
+    for copy in firsts:
+        copy.start()
     stay_slots = staying(slot, S, S - L)
     passes = [
-        pltpu.make_async_copy(stay.at[i], final.at[stay_slots[i]], stay_sem.at[i])
+        pltpu.make_async_copy(stay_v.at[i], final.at[stay_slots[i]], stay_sem.at[i])
         for i in range(S - L)
     ] + [
-        pltpu.make_async_copy(att_in, att, pass_sem.at[0]),
-        pltpu.make_async_copy(fconv_in, fconv, pass_sem.at[1]),
-        pltpu.make_async_copy(m_one, out.at[0], pass_sem.at[2]),
+        pltpu.make_async_copy(att_v, att, pass_sem.at[0]),
+        pltpu.make_async_copy(fconv_v, fconv, pass_sem.at[1]),
+        pltpu.make_async_copy(m_v, out.at[0], pass_sem.at[2]),
     ]
-    for copy in passes:
-        copy.start()
     wide = lambda v, c: jnp.concatenate([v] * ((c.stop - c.start) // HD), axis=1)
     for load in loads:
         load.wait()
     rate[...] = jnp.exp(rate[...])
+    for copy in firsts:
+        copy.wait()
+    for copy in passes:
+        copy.start()
     for i in range(S - L):
         y[pl.ds(stay_slots[i], 1), :] = y_stay[i : i + 1]
     results = []
@@ -756,6 +784,11 @@
             vm((2, S, C), BF16),
             vm((S, C)),
             vm((S, C), BF16),
+            vm((S - L, N, C)),
+            vm((2, S, QW), BF16),
+            vm((3, S, C)),
+            vm((S, C), BF16),
+            dma((4,)),
             dma((8,)),
             dma((L,)),
             dma((S - L,)),

time: 172 us -> 79.3 us (0.46)
  Pallas kernels: 171 us -> 78.5 us
    pallas_call x1, Pallas kernels: 97.7 us -> 6.28 us  [shards(): pl.pallas_call(functools.partial(finish_kernel, (R, S, L)), in_specs=[SME...]
where the time goes in v5:
time: 79.3 us; the launch traced here: 79.2 us
  Pallas kernels  78.5 us (99%)
    pallas_call x1, Pallas kernels, shards(): pl.pallas_call(functools.partial(exchange_kernel, (R, T, S, L, H, KV)), o...  72.2 us
    pallas_call x1, Pallas kernels, shards(): pl.pallas_call(functools.partial(finish_kernel, (R, S, L)), in_specs=[SME...  6.28 us

profile of v5, /device:TPU:0, one launch (start us, length us, event | category | flops | bytes accessed | tf_op | source)
XLA Modules:
  0.0 79.2 jit_solution(15962977111391997220)
XLA Ops:
  0.6 72.2 %exchange.1 = (f32[8,16,4096]{2,1,0:T(8,128)}, bf16[15,16,4096]{2,1,0:T(8,128)(2,1)}, bf16[2,16,2048]{2,1,0:T(8,128)(2,1)}, f32[3,16,4096]{2,1,0:T(8,128)}, bf16...) custom-call(s32[2,128]{1,0:T(2,128)} %bitcast.14, ...), custom_call_target="tpu_custom_call" | custom-call | tf_op jit(solution)/shard_map/exchange/pallas_call | solution.py:706
  72.9 6.3 %finish.1 = (bf16[2,16,2048]{2,1,0:T(8,128)(2,1)}, bf16[2,16,4096]{2,1,0:T(8,128)(2,1)}, f32[16,16,4096]{2,1,0:T(8,128)}, f32[3,16,4096]{2,1,0:T(8,128)}) custom-call(s32[2,128]{1,0:T(2,128)} %bitcast.15, f32[8,16,4096]{2,1,0:T(8,128)} %get-tuple-element.18.stay, bf16[15,16,4096]{2,1,0:T(8,128)(2,1)} %get-tuple-element.19.got_state, ...), custom_call_target="tpu_custom_call" | custom-call | tf_op jit(solution)/shard_map/finish/pallas_call | solution.py:764

commit v6 on v5

--- a/solution.py
+++ b/solution.py
@@ -223,7 +223,7 @@
     pl.semaphore_wait(barrier, R - 1 + T - 1)
 
     def lane(i):
-        return 1 + lax.rem(7 * i, R - 1)
+        return 1 + lax.rem(7 * i + 4 * me, R - 1)
 
     def send_states(i, _):
         k = lane(i)

time: 79.3 us -> 79.8 us (level)
  no operation moved by 1% of the time
where the time goes in v6:
time: 79.8 us; the launch traced here: 79.6 us
  Pallas kernels  79 us (99%)
    pallas_call x1, Pallas kernels, shards(): pl.pallas_call(functools.partial(exchange_kernel, (R, T, S, L, H, KV)), o...  72.7 us
    pallas_call x1, Pallas kernels, shards(): pl.pallas_call(functools.partial(finish_kernel, (R, S, L)), in_specs=[SME...  6.28 us

profile of v6, /device:TPU:0, one launch (start us, length us, event | category | flops | bytes accessed | tf_op | source)
XLA Modules:
  0.0 79.6 jit_solution(7377962460160696614)
XLA Ops:
  0.6 72.7 %exchange.1 = (f32[8,16,4096]{2,1,0:T(8,128)}, bf16[15,16,4096]{2,1,0:T(8,128)(2,1)}, bf16[2,16,2048]{2,1,0:T(8,128)(2,1)}, f32[3,16,4096]{2,1,0:T(8,128)}, bf16...) custom-call(s32[2,128]{1,0:T(2,128)} %bitcast.14, ...), custom_call_target="tpu_custom_call" | custom-call | tf_op jit(solution)/shard_map/exchange/pallas_call | solution.py:706
  73.4 6.3 %finish.1 = (bf16[2,16,2048]{2,1,0:T(8,128)(2,1)}, bf16[2,16,4096]{2,1,0:T(8,128)(2,1)}, f32[16,16,4096]{2,1,0:T(8,128)}, f32[3,16,4096]{2,1,0:T(8,128)}) custom-call(s32[2,128]{1,0:T(2,128)} %bitcast.15, f32[8,16,4096]{2,1,0:T(8,128)} %get-tuple-element.18.stay, bf16[15,16,4096]{2,1,0:T(8,128)(2,1)} %get-tuple-element.19.got_state, ...), custom_call_target="tpu_custom_call" | custom-call | tf_op jit(solution)/shard_map/finish/pallas_call | solution.py:764
